TPU v7x, 512 devices: a whole 4x4x16 slice. The times are simulated.
512 devices in a mesh: resp: 16 (over x, z_lo), pre: 16 (over y, z_hi), head: 2 (over core).
Axes of the slice: x: 4, y: 4, z: 16 (z_hi: 4, z_lo: 4; z = z_hi * 4 + z_lo), core: 2. Of those that a mesh axis runs over, the one named last changes fastest.
Arguments:
- queries: bfloat16 [16, 2048, 4096], P('resp', 'pre', 'head'), may hold values from -12 to 12
- keys: bfloat16 [16, 2048, 512], P('resp', 'pre', 'head'), may hold values from -12 to 12
- values: bfloat16 [16, 2048, 512], P('resp', 'pre', 'head'), may hold values from -6 to 6
- prefix_keys: bfloat16 [512, 512], P(('resp', 'pre'), 'head'), may hold values from -12 to 12
- prefix_values: bfloat16 [512, 512], P(('resp', 'pre'), 'head'), may hold values from -6 to 6
- grad_out: bfloat16 [16, 2048, 4096], P('resp', ('pre', 'head')), may hold values from -6 to 6
- lengths: int32 [16], P('resp'), may hold values from 256 to 2048, as said below
Outputs:
- grad_queries: bfloat16 [16, 2048, 4096], P('resp', ('pre', 'head'))
- grad_keys: bfloat16 [16, 2048, 512], P('resp', ('pre', 'head'))
- grad_values: bfloat16 [16, 2048, 512], P('resp', ('pre', 'head'))
- grad_prefix_keys: bfloat16 [512, 512], P(('resp', 'pre'), 'head')
- grad_prefix_values: bfloat16 [512, 512], P(('resp', 'pre'), 'head')
Inputs may be any that keep to these rules, and one draw needn't show every extreme that they name: `lengths`: one response has all 2048 positions live in every draw.
All inputs are finite; a program needn't handle non-finite values.
Results may differ from a plain program's by a relative error of at most 0.0075.
Values may be sent and summed in bfloat16 or wider, within the bound.
A program may use at most 64 MiB of HBM per device.

v0:
```python
import math

import jax
import jax.numpy as jnp
from jax import lax
from jax.sharding import PartitionSpec as P

HD = 128


SOFTCAP = 50.0


def passed_along(block, axis, distance):
    devices = range(lax.axis_size(axis))
    route = [((i - distance) % len(devices), i) for i in devices]
    return lax.ppermute(block, axis, route)


def split_heads(kv_rows, groups, head_dim):
    half_width = kv_rows.shape[1] // 2
    key_part = kv_rows[:, :half_width].reshape(kv_rows.shape[0], groups, head_dim)
    value_part = kv_rows[:, half_width:].reshape(kv_rows.shape[0], groups, head_dim)
    return (key_part, value_part)


def tangents(query_heads, key_part, head_dim):
    raw_score = jnp.einsum(
        "igkd,jgd->gkij", query_heads, key_part, preferred_element_type=jnp.float32
    )
    return jnp.tanh(raw_score * (1.0 / (math.sqrt(head_dim) * SOFTCAP)))


def first_pass(running, query_heads, kv_rows, visible, head_dim):
    totals, weighted = running
    key_part, value_part = split_heads(kv_rows, query_heads.shape[1], head_dim)
    tangent = tangents(query_heads, key_part, head_dim)
    weights = jnp.where(visible, jnp.exp(SOFTCAP * tangent), 0.0)
    weighted = weighted + jnp.einsum(
        "gkij,jgd->gkid",
        weights.astype(jnp.bfloat16),
        value_part,
        preferred_element_type=jnp.float32,
    )
    return (totals + jnp.sum(weights, axis=3), weighted)


def second_pass(query_heads, grad_heads, kv_rows, visible, log_total, row_dot, head_dim):
    key_part, value_part = split_heads(kv_rows, query_heads.shape[1], head_dim)
    tangent = tangents(query_heads, key_part, head_dim)
    probs = jnp.where(visible, jnp.exp(SOFTCAP * tangent - log_total[..., None]), 0.0)
    grad_probs = jnp.einsum(
        "igkd,jgd->gkij", grad_heads, value_part, preferred_element_type=jnp.float32
    )
    grad_score = (
        probs
        * (grad_probs - row_dot[..., None])
        * (1.0 - tangent * tangent)
        * (1.0 / math.sqrt(head_dim))
    ).astype(jnp.bfloat16)
    grad_query = jnp.einsum(
        "gkij,jgd->igkd", grad_score, key_part, preferred_element_type=jnp.float32
    )
    grad_key = jnp.einsum(
        "gkij,igkd->jgd", grad_score, query_heads, preferred_element_type=jnp.float32
    )
    grad_value = jnp.einsum(
        "gkij,igkd->jgd", probs.astype(jnp.bfloat16), grad_heads, preferred_element_type=jnp.float32
    )
    row_count = kv_rows.shape[0]
    return (
        grad_query,
        jnp.concatenate(
            [grad_key.reshape(row_count, -1), grad_value.reshape(row_count, -1)], axis=1
        ),
    )


def shards(queries, keys, values, prefix_keys, prefix_values, grad_out, lengths):
    grad_here = lax.all_to_all(grad_out, "head", split_axis=2, concat_axis=1, tiled=True)
    row_count = queries.shape[1]
    head_count = queries.shape[2] // HD
    groups = keys.shape[2] // HD
    per_group = head_count // groups
    query_heads = queries[0].reshape(row_count, groups, per_group, HD)
    my_place = lax.axis_index("pre")
    cycle_size = lax.axis_size("pre")
    length = lengths[0]
    query_pos = my_place * row_count + jnp.arange(row_count, dtype=jnp.int32)
    is_live = query_pos < length
    grad_rows = jnp.where(is_live[:, None], grad_here[0], jnp.zeros_like(grad_here[0]))
    grad_heads = grad_rows.reshape(row_count, groups, per_group, HD)
    own_rows = jnp.concatenate([keys[0], values[0]], axis=1)
    kv_width = own_rows.shape[1]
    half_width = kv_width // 2
    prompt_own = jnp.concatenate([prefix_keys, prefix_values], axis=1)
    prompt_rows = lax.all_gather(prompt_own, "resp", axis=0, tiled=True)
    key_block = jnp.concatenate([own_rows, prompt_rows], axis=0)

    def fetch_block(block_rows):
        return passed_along(block_rows, "pre", 1)

    def response_visible(source):
        key_pos = source * row_count + jnp.arange(row_count, dtype=jnp.int32)
        return (key_pos[None, :] <= query_pos[:, None]) & (key_pos[None, :] < length)

    def has_work(source):
        return (source <= my_place) & (source * row_count < length)

    def all_visible(width):
        return jnp.ones((row_count, width), dtype=bool)

    def pass_grads(partial_rows):
        return passed_along(partial_rows, "pre", 1)

    def stats_step(running, block_rows, source):
        running = lax.cond(
            has_work(source),
            lambda state: first_pass(
                state, query_heads, block_rows[:row_count], response_visible(source), HD
            ),
            lambda state: state,
            running,
        )
        running = first_pass(
            running,
            query_heads,
            block_rows[row_count:],
            all_visible(block_rows.shape[0] - row_count),
            HD,
        )
        return running

    running = (
        jnp.zeros((groups, per_group, row_count), jnp.float32),
        jnp.zeros((groups, per_group, row_count, HD), jnp.float32),
    )
    running = stats_step(running, key_block, my_place)

    def stats_loop(step, state):
        block_rows, running = state
        source = (my_place - step) % cycle_size
        block_rows = fetch_block(block_rows)
        return (block_rows, stats_step(running, block_rows, source))

    _, running = lax.fori_loop(1, cycle_size, stats_loop, (key_block, running))
    totals, weighted = running
    log_total = jnp.log(totals)
    attn_out = weighted / totals[..., None]
    row_dot = jnp.sum(
        jnp.transpose(grad_heads, (1, 2, 0, 3)).astype(jnp.float32) * attn_out, axis=3
    )

    def grad_step(grad_query, block_rows, source):

        def working(current):
            query_term, block_term = second_pass(
                query_heads,
                grad_heads,
                block_rows[:row_count],
                response_visible(source),
                log_total,
                row_dot,
                HD,
            )
            return (current + query_term, block_term)

        def resting(current):
            return (current, jnp.zeros((row_count, kv_width), jnp.float32))

        grad_query, response_term = lax.cond(has_work(source), working, resting, grad_query)
        query_term, prompt_term = second_pass(
            query_heads,
            grad_heads,
            block_rows[row_count:],
            all_visible(block_rows.shape[0] - row_count),
            log_total,
            row_dot,
            HD,
        )
        return (grad_query + query_term, jnp.concatenate([response_term, prompt_term], axis=0))

    grad_query = jnp.zeros((row_count, groups, per_group, HD), jnp.float32)
    grad_query, travel = grad_step(grad_query, key_block, my_place)

    def grad_loop(step, state):
        block_rows, travel, grad_query = state
        source = (my_place - step) % cycle_size
        block_rows = fetch_block(block_rows)
        travel = pass_grads(travel)
        grad_query, block_term = grad_step(grad_query, block_rows, source)
        return (block_rows, travel + block_term, grad_query)

    _, travel, grad_query = lax.fori_loop(1, cycle_size, grad_loop, (key_block, travel, grad_query))
    travel = pass_grads(travel)
    prompt_total = lax.psum_scatter(travel[row_count:], "resp", scatter_dimension=0, tiled=True)
    query_out = grad_query.reshape(row_count, head_count * HD).astype(jnp.bfloat16)[None]
    key_out = travel[:row_count, :half_width].astype(jnp.bfloat16)[None]
    value_out = travel[:row_count, half_width:].astype(jnp.bfloat16)[None]
    query_back, key_back, value_back = (
        lax.all_to_all(query_out, "head", split_axis=1, concat_axis=2, tiled=True),
        lax.all_to_all(key_out, "head", split_axis=1, concat_axis=2, tiled=True),
        lax.all_to_all(value_out, "head", split_axis=1, concat_axis=2, tiled=True),
    )
    return (
        query_back,
        key_back,
        value_back,
        prompt_total[:, :half_width].astype(jnp.bfloat16),
        prompt_total[:, half_width:].astype(jnp.bfloat16),
    )


def solution(mesh):
    in_specs = (
        P("resp", "pre", "head"),
        P("resp", "pre", "head"),
        P("resp", "pre", "head"),
        P(("resp", "pre"), "head"),
        P(("resp", "pre"), "head"),
        P("resp", ("pre", "head"), None),
        P("resp"),
    )
    out_specs = (
        P("resp", ("pre", "head"), None),
        P("resp", ("pre", "head"), None),
        P("resp", ("pre", "head"), None),
        P(("resp", "pre"), "head"),
        P(("resp", "pre"), "head"),
    )
    return jax.shard_map(shards, mesh=mesh, in_specs=in_specs, out_specs=out_specs, check_vma=False)
```

profile of v0, /device:TPU:1, one launch (start us, length us, event | category | flops | bytes accessed | tf_op | source)
XLA Modules:
  0.0 1872.3 jit_solution(1224665055126485827)
XLA Ops:
  6.0 23.3 %reduce = bf16[4096,64]{1,0:T(8,128)(2,1)} reduce(bf16[4096,1,64]{2,1,0:T(2,128)(2,1)S(1)} %bitcast.384, bf16[]{:T(256)} %broadcast.286), dimensions={1}, to_apply=%bitcast.267.reduce_sub_computation | reduce | bytes 1048578
  32.0 11.2 all-to-all-start
  43.2 31.1 %all-gather = bf16[16,2,512]{2,1,0:T(2,128)(2,1)S(1)} all-gather(bf16[1,2,512]{2,1,0:T(2,128)(2,1)S(1)} %maximum_bitcast_fusion), channel_id=1, replica_groups=mesh['resp'=16,'pre'=16,'head'=2] {'resp'}, dimensions={0}, use_global_device_ids=true | all-gather | bytes 34816 | tf_op jit(solution)/shard_map/all_gather | solution.py:97
  80.8 505.7 %while.43 = (s32[]{:T(128)}, bf16[160,512]{0,1:T(8,128)(2,1)}, f32[2,8,128]{2,1,0:T(8,128)S(1)}, f32[2,8,128,128]{3,2,1,0:T(8,128)S(1)}, s32[]{:T(128)}, /*index...) while((s32[]{:T(128)}, bf16[160,512]{0,1:T(8,128)(2,1)}, ...), condition=%wide.region_9.10_spmd.clone, body=%wide.region_4.9_spmd.clone.sunk | while | flops 169902608 | bytes 10227400 | solution.py:146
  80.8 8.8 collective-permute-start
  90.3 11.2 collective-permute-done
  103.8 10.5 collective-permute-start
  115.0 9.6 collective-permute-done
  135.3 11.0 collective-permute-done
  157.0 20.9 %collective-permute-done = bf16[160,512]{0,1:T(8,128)(2,1)S(1)} collective-permute-done((bf16[160,512]{0,1:T(8,128)(2,1)}, bf16[160,512]{0,1:T(8,128)(2,1)S(1)}, u32[]{:S(2)}, u32[]{:S(2)}) %collective-permute-start) | collective-permute-done | bytes 163872 | tf_op jit(solution)/shard_map/while/body/eval_jaxpr/ppermute | solution.py:17
  188.8 14.2 collective-permute-done
  207.9 29.0 %collective-permute-done = bf16[160,512]{0,1:T(8,128)(2,1)S(1)} collective-permute-done((bf16[160,512]{0,1:T(8,128)(2,1)}, bf16[160,512]{0,1:T(8,128)(2,1)S(1)}, u32[]{:S(2)}, u32[]{:S(2)}) %collective-permute-start) | collective-permute-done | bytes 163872 | tf_op jit(solution)/shard_map/while/body/eval_jaxpr/ppermute | solution.py:17
  239.2 10.1 collective-permute-start
  250.0 15.5 collective-permute-done
  267.8 67.3 %collective-permute-start = (bf16[160,512]{0,1:T(8,128)(2,1)}, bf16[160,512]{0,1:T(8,128)(2,1)S(1)}, u32[]{:S(2)}, u32[]{:S(2)}) collective-permute-start(bf16[160,512]{0,1:T(8,128)(2,1)} %get-tuple-element.1077), channel_id=1, source_target_pairs={{30,0},{0,2},{2,4},{4,6},{6,8},{8,10},{10,12},{12,14},{14,16},{16,... | collective-permute-start | bytes 491528 | tf_op jit(solution)/shard_map/while/body/eval_jaxpr/ppermute | solution.py:17
  335.8 19.5 %collective-permute-done = bf16[160,512]{0,1:T(8,128)(2,1)S(1)} collective-permute-done((bf16[160,512]{0,1:T(8,128)(2,1)}, bf16[160,512]{0,1:T(8,128)(2,1)S(1)}, u32[]{:S(2)}, u32[]{:S(2)}) %collective-permute-start) | collective-permute-done | bytes 163872 | tf_op jit(solution)/shard_map/while/body/eval_jaxpr/ppermute | solution.py:17
  366.2 12.6 collective-permute-done
  387.8 12.0 collective-permute-done
  404.7 19.7 %collective-permute-done = bf16[160,512]{0,1:T(8,128)(2,1)S(1)} collective-permute-done((bf16[160,512]{0,1:T(8,128)(2,1)}, bf16[160,512]{0,1:T(8,128)(2,1)S(1)}, u32[]{:S(2)}, u32[]{:S(2)}) %collective-permute-start) | collective-permute-done | bytes 163872 | tf_op jit(solution)/shard_map/while/body/eval_jaxpr/ppermute | solution.py:17
  426.7 13.6 collective-permute-start
  446.3 12.9 collective-permute-start
  467.3 21.2 %collective-permute-start = (bf16[160,512]{0,1:T(8,128)(2,1)}, bf16[160,512]{0,1:T(8,128)(2,1)S(1)}, u32[]{:S(2)}, u32[]{:S(2)}) collective-permute-start(bf16[160,512]{0,1:T(8,128)(2,1)} %get-tuple-element.1077), channel_id=1, source_target_pairs={{30,0},{0,2},{2,4},{4,6},{6,8},{8,10},{10,12},{12,14},{14,16},{16,... | collective-permute-start | bytes 491528 | tf_op jit(solution)/shard_map/while/body/eval_jaxpr/ppermute | solution.py:17
  489.1 30.8 %collective-permute-done = bf16[160,512]{0,1:T(8,128)(2,1)S(1)} collective-permute-done((bf16[160,512]{0,1:T(8,128)(2,1)}, bf16[160,512]{0,1:T(8,128)(2,1)S(1)}, u32[]{:S(2)}, u32[]{:S(2)}) %collective-permute-start) | collective-permute-done | bytes 163872 | tf_op jit(solution)/shard_map/while/body/eval_jaxpr/ppermute | solution.py:17
  522.2 13.0 collective-permute-start
  536.0 48.2 %collective-permute-done = bf16[160,512]{0,1:T(8,128)(2,1)S(1)} collective-permute-done((bf16[160,512]{0,1:T(8,128)(2,1)}, bf16[160,512]{0,1:T(8,128)(2,1)S(1)}, u32[]{:S(2)}, u32[]{:S(2)}) %collective-permute-start) | collective-permute-done | bytes 163872 | tf_op jit(solution)/shard_map/while/body/eval_jaxpr/ppermute | solution.py:17
  599.3 9.3 conditional.5
  615.0 1101.9 %while.44 = (s32[]{:T(128)}, bf16[160,512]{0,1:T(8,128)(2,1)S(1)}, f32[160,512]{0,1:T(8,128)}, f32[128,2,8,128]{3,0,2,1:T(8,128)S(1)}, s32[]{:T(128)}, /*index=5...) while((s32[]{:T(128)}, bf16[160,512]{0,1:T(8,128)(2,1)S(1)}, ...), condition=%wide.region_16.17_spmd.clone, body=%wide.region_13.16_spmd.clone.sunk | while | flops 425017856 | bytes 21581568 | solution.py:194
  619.5 29.4 %collective-permute-done.1 = bf16[160,512]{0,1:T(8,128)(2,1)S(1)} collective-permute-done((bf16[160,512]{0,1:T(8,128)(2,1)S(1)}, bf16[160,512]{0,1:T(8,128)(2,1)S(1)}, u32[]{:S(2)}, u32[]{:S(2)}) %collective-permute-start.1) | collective-permute-done | bytes 163872 | tf_op jit(solution)/shard_map/while/body/eval_jaxpr/ppermute | solution.py:17
  650.9 31.0 %collective-permute-done.2 = f32[160,512]{0,1:T(8,128)} collective-permute-done((f32[160,512]{0,1:T(8,128)}, f32[160,512]{0,1:T(8,128)}, u32[]{:S(2)}, u32[]{:S(2)}) %collective-permute-start.2) | collective-permute-done | bytes 327712 | tf_op jit(solution)/shard_map/while/body/eval_jaxpr/ppermute | solution.py:17
  685.6 17.2 collective-permute-start.2
  705.5 28.0 %collective-permute-done.2 = f32[160,512]{0,1:T(8,128)} collective-permute-done((f32[160,512]{0,1:T(8,128)}, f32[160,512]{0,1:T(8,128)}, u32[]{:S(2)}, u32[]{:S(2)}) %collective-permute-start.2) | collective-permute-done | bytes 327712 | tf_op jit(solution)/shard_map/while/body/eval_jaxpr/ppermute | solution.py:17
  735.4 19.6 %collective-permute-start.1 = (bf16[160,512]{0,1:T(8,128)(2,1)S(1)}, bf16[160,512]{0,1:T(8,128)(2,1)S(1)}, u32[]{:S(2)}, u32[]{:S(2)}) collective-permute-start(bf16[160,512]{0,1:T(8,128)(2,1)S(1)} %get-tuple-element.1123), channel_id=1, source_target_pairs={{30,0},{0,2},{2,4},{4,6},{6,8},{8,10},{10,12},{12,14},{14,16},{16,... | collective-permute-start | bytes 491528 | tf_op jit(solution)/shard_map/while/body/eval_jaxpr/ppermute | solution.py:17
  755.0 8.0 collective-permute-start.2
  763.7 12.1 collective-permute-done.1
  777.8 85.1 %collective-permute-done.2 = f32[160,512]{0,1:T(8,128)} collective-permute-done((f32[160,512]{0,1:T(8,128)}, f32[160,512]{0,1:T(8,128)}, u32[]{:S(2)}, u32[]{:S(2)}) %collective-permute-start.2) | collective-permute-done | bytes 327712 | tf_op jit(solution)/shard_map/while/body/eval_jaxpr/ppermute | solution.py:17
  869.3 28.4 %collective-permute-done.1 = bf16[160,512]{0,1:T(8,128)(2,1)S(1)} collective-permute-done((bf16[160,512]{0,1:T(8,128)(2,1)S(1)}, bf16[160,512]{0,1:T(8,128)(2,1)S(1)}, u32[]{:S(2)}, u32[]{:S(2)}) %collective-permute-start.1) | collective-permute-done | bytes 163872 | tf_op jit(solution)/shard_map/while/body/eval_jaxpr/ppermute | solution.py:17
  899.6 68.7 %collective-permute-done.2 = f32[160,512]{0,1:T(8,128)} collective-permute-done((f32[160,512]{0,1:T(8,128)}, f32[160,512]{0,1:T(8,128)}, u32[]{:S(2)}, u32[]{:S(2)}) %collective-permute-start.2) | collective-permute-done | bytes 327712 | tf_op jit(solution)/shard_map/while/body/eval_jaxpr/ppermute | solution.py:17
  970.2 8.0 collective-permute-start.1
  980.8 17.9 collective-permute-done.1
  1000.7 19.5 %collective-permute-done.2 = f32[160,512]{0,1:T(8,128)} collective-permute-done((f32[160,512]{0,1:T(8,128)}, f32[160,512]{0,1:T(8,128)}, u32[]{:S(2)}, u32[]{:S(2)}) %collective-permute-start.2) | collective-permute-done | bytes 327712 | tf_op jit(solution)/shard_map/while/body/eval_jaxpr/ppermute | solution.py:17
  1026.6 37.4 %collective-permute-done.1 = bf16[160,512]{0,1:T(8,128)(2,1)S(1)} collective-permute-done((bf16[160,512]{0,1:T(8,128)(2,1)S(1)}, bf16[160,512]{0,1:T(8,128)(2,1)S(1)}, u32[]{:S(2)}, u32[]{:S(2)}) %collective-permute-start.1) | collective-permute-done | bytes 163872 | tf_op jit(solution)/shard_map/while/body/eval_jaxpr/ppermute | solution.py:17
  1066.1 9.4 collective-permute-done.2
  1083.1 47.9 %collective-permute-done.1 = bf16[160,512]{0,1:T(8,128)(2,1)S(1)} collective-permute-done((bf16[160,512]{0,1:T(8,128)(2,1)S(1)}, bf16[160,512]{0,1:T(8,128)(2,1)S(1)}, u32[]{:S(2)}, u32[]{:S(2)}) %collective-permute-start.1) | collective-permute-done | bytes 163872 | tf_op jit(solution)/shard_map/while/body/eval_jaxpr/ppermute | solution.py:17
  1133.0 13.6 collective-permute-done.2
  1153.0 11.1 collective-permute-done.1
  1166.0 9.5 collective-permute-done.2
  1181.9 48.8 %collective-permute-done.1 = bf16[160,512]{0,1:T(8,128)(2,1)S(1)} collective-permute-done((bf16[160,512]{0,1:T(8,128)(2,1)S(1)}, bf16[160,512]{0,1:T(8,128)(2,1)S(1)}, u32[]{:S(2)}, u32[]{:S(2)}) %collective-permute-start.1) | collective-permute-done | bytes 163872 | tf_op jit(solution)/shard_map/while/body/eval_jaxpr/ppermute | solution.py:17
  1232.6 15.1 collective-permute-done.2
  1254.1 71.3 %collective-permute-done.1 = bf16[160,512]{0,1:T(8,128)(2,1)S(1)} collective-permute-done((bf16[160,512]{0,1:T(8,128)(2,1)S(1)}, bf16[160,512]{0,1:T(8,128)(2,1)S(1)}, u32[]{:S(2)}, u32[]{:S(2)}) %collective-permute-start.1) | collective-permute-done | bytes 163872 | tf_op jit(solution)/shard_map/while/body/eval_jaxpr/ppermute | solution.py:17
  1327.4 13.5 collective-permute-done.2
  1342.8 137.5 %collective-permute-start.1 = (bf16[160,512]{0,1:T(8,128)(2,1)S(1)}, bf16[160,512]{0,1:T(8,128)(2,1)S(1)}, u32[]{:S(2)}, u32[]{:S(2)}) collective-permute-start(bf16[160,512]{0,1:T(8,128)(2,1)S(1)} %get-tuple-element.1123), channel_id=1, source_target_pairs={{30,0},{0,2},{2,4},{4,6},{6,8},{8,10},{10,12},{12,14},{14,16},{16,... | collective-permute-start | bytes 491528 | tf_op jit(solution)/shard_map/while/body/eval_jaxpr/ppermute | solution.py:17
  1480.3 8.0 collective-permute-start.2
  1489.0 12.7 collective-permute-done.1
  1503.7 35.9 %collective-permute-done.2 = f32[160,512]{0,1:T(8,128)} collective-permute-done((f32[160,512]{0,1:T(8,128)}, f32[160,512]{0,1:T(8,128)}, u32[]{:S(2)}, u32[]{:S(2)}) %collective-permute-start.2) | collective-permute-done | bytes 327712 | tf_op jit(solution)/shard_map/while/body/eval_jaxpr/ppermute | solution.py:17
  1548.7 12.6 collective-permute-done.1
  1563.3 14.5 collective-permute-done.2
  1584.2 9.7 collective-permute-done.1
  1595.9 9.4 collective-permute-done.2
  1613.2 57.9 %collective-permute-done.1 = bf16[160,512]{0,1:T(8,128)(2,1)S(1)} collective-permute-done((bf16[160,512]{0,1:T(8,128)(2,1)S(1)}, bf16[160,512]{0,1:T(8,128)(2,1)S(1)}, u32[]{:S(2)}, u32[]{:S(2)}) %collective-permute-start.1) | collective-permute-done | bytes 163872 | tf_op jit(solution)/shard_map/while/body/eval_jaxpr/ppermute | solution.py:17
  1673.1 9.4 collective-permute-done.2
  1688.9 11.9 collective-permute-done.1
  1702.8 12.2 collective-permute-done.2
  1747.2 10.4 all_to_all.69
  1763.9 107.8 %all-reduce = bf16[32,512]{1,0:T(8,128)(2,1)S(1)} all-reduce(f32[32,512]{1,0:T(8,128)S(1)} %slice.114), channel_id=2, replica_groups=mesh['resp'=16,'pre'=16,'head'=2] {'resp'}, use_global_device_ids=true, to_apply=%region_17.18.clone | all-reduce | flops 16384 | bytes 98304
  (514 shorter events, 271.7 us)
Async XLA Ops:
  29.3 13.9 copy-start.18
  29.3 13.9 copy-start.19
  29.3 45.2 %copy-start.9 = (bf16[1,128,2048]{2,1,0:T(8,128)(2,1)S(1)}, bf16[1,128,2048]{2,1,0:T(8,128)(2,1)}, u32[]{:S(2)}) copy-start(bf16[1,128,2048]{2,1,0:T(8,128)(2,1)} %param.19) | copy-start | bytes 1572868
  32.0 44.7 %copy-start.7 = (bf16[1,128,256]{2,1,0:T(8,128)(2,1)S(1)}, bf16[1,128,256]{2,1,0:T(8,128)(2,1)}, u32[]{:S(2)}) copy-start(bf16[1,128,256]{2,1,0:T(8,128)(2,1)} %param.20) | copy-start | bytes 196612
  32.0 44.9 %copy-start.6 = (bf16[1,128,256]{2,1,0:T(8,128)(2,1)S(1)}, bf16[1,128,256]{2,1,0:T(8,128)(2,1)}, u32[]{:S(2)}) copy-start(bf16[1,128,256]{2,1,0:T(8,128)(2,1)} %param.21) | copy-start | bytes 196612
  32.0 554.6 %all-to-all-start = ((bf16[2,2,65536]{2,1,0:T(2,128)(2,1)}), bf16[2,2,65536]{2,1,0:T(2,128)(2,1)}, u32[]{:S(2)}, u32[]{:S(2)}) async-start(bf16[2,2,65536]{2,1,0:T(2,128)(2,1)} %reshape.218), calls=%async_computation | async-start | bytes 1048576 | tf_op jit(solution)/shard_map/all_to_all | solution.py:80
  74.5 3.2 copy-start.16
  76.0 3.7 copy-start
  80.8 20.7 %collective-permute-start = (bf16[160,512]{0,1:T(8,128)(2,1)}, bf16[160,512]{0,1:T(8,128)(2,1)S(1)}, u32[]{:S(2)}, u32[]{:S(2)}) collective-permute-start(bf16[160,512]{0,1:T(8,128)(2,1)} %get-tuple-element.1077), channel_id=1, source_target_pairs={{30,0},{0,2},{2,4},{4,6},{6,8},{8,10},{10,12},{12,14},{14,16},{16,... | collective-permute-start | bytes 491528 | tf_op jit(solution)/shard_map/while/body/eval_jaxpr/ppermute | solution.py:17
  103.8 20.9 %collective-permute-start = (bf16[160,512]{0,1:T(8,128)(2,1)}, bf16[160,512]{0,1:T(8,128)(2,1)S(1)}, u32[]{:S(2)}, u32[]{:S(2)}) collective-permute-start(bf16[160,512]{0,1:T(8,128)(2,1)} %get-tuple-element.1077), channel_id=1, source_target_pairs={{30,0},{0,2},{2,4},{4,6},{6,8},{8,10},{10,12},{12,14},{14,16},{16,... | collective-permute-start | bytes 491528 | tf_op jit(solution)/shard_map/while/body/eval_jaxpr/ppermute | solution.py:17
  126.9 19.4 %collective-permute-start = (bf16[160,512]{0,1:T(8,128)(2,1)}, bf16[160,512]{0,1:T(8,128)(2,1)S(1)}, u32[]{:S(2)}, u32[]{:S(2)}) collective-permute-start(bf16[160,512]{0,1:T(8,128)(2,1)} %get-tuple-element.1077), channel_id=1, source_target_pairs={{30,0},{0,2},{2,4},{4,6},{6,8},{8,10},{10,12},{12,14},{14,16},{16,... | collective-permute-start | bytes 491528 | tf_op jit(solution)/shard_map/while/body/eval_jaxpr/ppermute | solution.py:17
  148.6 29.3 %collective-permute-start = (bf16[160,512]{0,1:T(8,128)(2,1)}, bf16[160,512]{0,1:T(8,128)(2,1)S(1)}, u32[]{:S(2)}, u32[]{:S(2)}) collective-permute-start(bf16[160,512]{0,1:T(8,128)(2,1)} %get-tuple-element.1077), channel_id=1, source_target_pairs={{30,0},{0,2},{2,4},{4,6},{6,8},{8,10},{10,12},{12,14},{14,16},{16,... | collective-permute-start | bytes 491528 | tf_op jit(solution)/shard_map/while/body/eval_jaxpr/ppermute | solution.py:17
  180.2 22.8 %collective-permute-start = (bf16[160,512]{0,1:T(8,128)(2,1)}, bf16[160,512]{0,1:T(8,128)(2,1)S(1)}, u32[]{:S(2)}, u32[]{:S(2)}) collective-permute-start(bf16[160,512]{0,1:T(8,128)(2,1)} %get-tuple-element.1077), channel_id=1, source_target_pairs={{30,0},{0,2},{2,4},{4,6},{6,8},{8,10},{10,12},{12,14},{14,16},{16,... | collective-permute-start | bytes 491528 | tf_op jit(solution)/shard_map/while/body/eval_jaxpr/ppermute | solution.py:17
  205.3 31.6 %collective-permute-start = (bf16[160,512]{0,1:T(8,128)(2,1)}, bf16[160,512]{0,1:T(8,128)(2,1)S(1)}, u32[]{:S(2)}, u32[]{:S(2)}) collective-permute-start(bf16[160,512]{0,1:T(8,128)(2,1)} %get-tuple-element.1077), channel_id=1, source_target_pairs={{30,0},{0,2},{2,4},{4,6},{6,8},{8,10},{10,12},{12,14},{14,16},{16,... | collective-permute-start | bytes 491528 | tf_op jit(solution)/shard_map/while/body/eval_jaxpr/ppermute | solution.py:17
  239.2 26.3 %collective-permute-start = (bf16[160,512]{0,1:T(8,128)(2,1)}, bf16[160,512]{0,1:T(8,128)(2,1)S(1)}, u32[]{:S(2)}, u32[]{:S(2)}) collective-permute-start(bf16[160,512]{0,1:T(8,128)(2,1)} %get-tuple-element.1077), channel_id=1, source_target_pairs={{30,0},{0,2},{2,4},{4,6},{6,8},{8,10},{10,12},{12,14},{14,16},{16,... | collective-permute-start | bytes 491528 | tf_op jit(solution)/shard_map/while/body/eval_jaxpr/ppermute | solution.py:17
  267.8 87.5 %collective-permute-start = (bf16[160,512]{0,1:T(8,128)(2,1)}, bf16[160,512]{0,1:T(8,128)(2,1)S(1)}, u32[]{:S(2)}, u32[]{:S(2)}) collective-permute-start(bf16[160,512]{0,1:T(8,128)(2,1)} %get-tuple-element.1077), channel_id=1, source_target_pairs={{30,0},{0,2},{2,4},{4,6},{6,8},{8,10},{10,12},{12,14},{14,16},{16,... | collective-permute-start | bytes 491528 | tf_op jit(solution)/shard_map/while/body/eval_jaxpr/ppermute | solution.py:17
  357.6 21.2 %collective-permute-start = (bf16[160,512]{0,1:T(8,128)(2,1)}, bf16[160,512]{0,1:T(8,128)(2,1)S(1)}, u32[]{:S(2)}, u32[]{:S(2)}) collective-permute-start(bf16[160,512]{0,1:T(8,128)(2,1)} %get-tuple-element.1077), channel_id=1, source_target_pairs={{30,0},{0,2},{2,4},{4,6},{6,8},{8,10},{10,12},{12,14},{14,16},{16,... | collective-permute-start | bytes 491528 | tf_op jit(solution)/shard_map/while/body/eval_jaxpr/ppermute | solution.py:17
  381.1 18.8 %collective-permute-start = (bf16[160,512]{0,1:T(8,128)(2,1)}, bf16[160,512]{0,1:T(8,128)(2,1)S(1)}, u32[]{:S(2)}, u32[]{:S(2)}) collective-permute-start(bf16[160,512]{0,1:T(8,128)(2,1)} %get-tuple-element.1077), channel_id=1, source_target_pairs={{30,0},{0,2},{2,4},{4,6},{6,8},{8,10},{10,12},{12,14},{14,16},{16,... | collective-permute-start | bytes 491528 | tf_op jit(solution)/shard_map/while/body/eval_jaxpr/ppermute | solution.py:17
  402.1 22.3 %collective-permute-start = (bf16[160,512]{0,1:T(8,128)(2,1)}, bf16[160,512]{0,1:T(8,128)(2,1)S(1)}, u32[]{:S(2)}, u32[]{:S(2)}) collective-permute-start(bf16[160,512]{0,1:T(8,128)(2,1)} %get-tuple-element.1077), channel_id=1, source_target_pairs={{30,0},{0,2},{2,4},{4,6},{6,8},{8,10},{10,12},{12,14},{14,16},{16,... | collective-permute-start | bytes 491528 | tf_op jit(solution)/shard_map/while/body/eval_jaxpr/ppermute | solution.py:17
  426.7 17.3 collective-permute-start
  446.3 18.7 collective-permute-start
  467.3 52.7 %collective-permute-start = (bf16[160,512]{0,1:T(8,128)(2,1)}, bf16[160,512]{0,1:T(8,128)(2,1)S(1)}, u32[]{:S(2)}, u32[]{:S(2)}) collective-permute-start(bf16[160,512]{0,1:T(8,128)(2,1)} %get-tuple-element.1077), channel_id=1, source_target_pairs={{30,0},{0,2},{2,4},{4,6},{6,8},{8,10},{10,12},{12,14},{14,16},{16,... | collective-permute-start | bytes 491528 | tf_op jit(solution)/shard_map/while/body/eval_jaxpr/ppermute | solution.py:17
  522.2 61.9 %collective-permute-start = (bf16[160,512]{0,1:T(8,128)(2,1)}, bf16[160,512]{0,1:T(8,128)(2,1)S(1)}, u32[]{:S(2)}, u32[]{:S(2)}) collective-permute-start(bf16[160,512]{0,1:T(8,128)(2,1)} %get-tuple-element.1077), channel_id=1, source_target_pairs={{30,0},{0,2},{2,4},{4,6},{6,8},{8,10},{10,12},{12,14},{14,16},{16,... | collective-permute-start | bytes 491528 | tf_op jit(solution)/shard_map/while/body/eval_jaxpr/ppermute | solution.py:17
  594.5 2.9 copy-start.1
  594.6 3.5 copy-start.15
  594.6 3.7 copy-start.17
  599.3 9.3 copy-start.14
  602.7 2.4 copy-start.2
  602.7 2.4 copy-start.10
  608.6 2.9 copy-start.8
  611.5 3.5 copy-start.4
  611.5 3.4 copy-start.12
  615.0 33.9 %collective-permute-start.1 = (bf16[160,512]{0,1:T(8,128)(2,1)S(1)}, bf16[160,512]{0,1:T(8,128)(2,1)S(1)}, u32[]{:S(2)}, u32[]{:S(2)}) collective-permute-start(bf16[160,512]{0,1:T(8,128)(2,1)S(1)} %get-tuple-element.1123), channel_id=1, source_target_pairs={{30,0},{0,2},{2,4},{4,6},{6,8},{8,10},{10,12},{12,14},{14,16},{16,... | collective-permute-start | bytes 491528 | tf_op jit(solution)/shard_map/while/body/eval_jaxpr/ppermute | solution.py:17
  616.9 65.0 %collective-permute-start.2 = (f32[160,512]{0,1:T(8,128)}, f32[160,512]{0,1:T(8,128)}, u32[]{:S(2)}, u32[]{:S(2)}) collective-permute-start(f32[160,512]{0,1:T(8,128)} %get-tuple-element.1124), channel_id=1, source_target_pairs={{30,0},{0,2},{2,4},{4,6},{6,8},{8,10},{10,12},{12,14},{14,16},{16,... | collective-permute-start | bytes 983048 | tf_op jit(solution)/shard_map/while/body/eval_jaxpr/ppermute | solution.py:17
  683.7 19.8 %collective-permute-start.1 = (bf16[160,512]{0,1:T(8,128)(2,1)S(1)}, bf16[160,512]{0,1:T(8,128)(2,1)S(1)}, u32[]{:S(2)}, u32[]{:S(2)}) collective-permute-start(bf16[160,512]{0,1:T(8,128)(2,1)S(1)} %get-tuple-element.1123), channel_id=1, source_target_pairs={{30,0},{0,2},{2,4},{4,6},{6,8},{8,10},{10,12},{12,14},{14,16},{16,... | collective-permute-start | bytes 491528 | tf_op jit(solution)/shard_map/while/body/eval_jaxpr/ppermute | solution.py:17
  685.6 47.8 %collective-permute-start.2 = (f32[160,512]{0,1:T(8,128)}, f32[160,512]{0,1:T(8,128)}, u32[]{:S(2)}, u32[]{:S(2)}) collective-permute-start(f32[160,512]{0,1:T(8,128)} %get-tuple-element.1124), channel_id=1, source_target_pairs={{30,0},{0,2},{2,4},{4,6},{6,8},{8,10},{10,12},{12,14},{14,16},{16,... | collective-permute-start | bytes 983048 | tf_op jit(solution)/shard_map/while/body/eval_jaxpr/ppermute | solution.py:17
  735.4 40.4 %collective-permute-start.1 = (bf16[160,512]{0,1:T(8,128)(2,1)S(1)}, bf16[160,512]{0,1:T(8,128)(2,1)S(1)}, u32[]{:S(2)}, u32[]{:S(2)}) collective-permute-start(bf16[160,512]{0,1:T(8,128)(2,1)S(1)} %get-tuple-element.1123), channel_id=1, source_target_pairs={{30,0},{0,2},{2,4},{4,6},{6,8},{8,10},{10,12},{12,14},{14,16},{16,... | collective-permute-start | bytes 491528 | tf_op jit(solution)/shard_map/while/body/eval_jaxpr/ppermute | solution.py:17
  755.0 107.9 %collective-permute-start.2 = (f32[160,512]{0,1:T(8,128)}, f32[160,512]{0,1:T(8,128)}, u32[]{:S(2)}, u32[]{:S(2)}) collective-permute-start(f32[160,512]{0,1:T(8,128)} %get-tuple-element.1124), channel_id=1, source_target_pairs={{30,0},{0,2},{2,4},{4,6},{6,8},{8,10},{10,12},{12,14},{14,16},{16,... | collective-permute-start | bytes 983048 | tf_op jit(solution)/shard_map/while/body/eval_jaxpr/ppermute | solution.py:17
  864.7 32.9 %collective-permute-start.1 = (bf16[160,512]{0,1:T(8,128)(2,1)S(1)}, bf16[160,512]{0,1:T(8,128)(2,1)S(1)}, u32[]{:S(2)}, u32[]{:S(2)}) collective-permute-start(bf16[160,512]{0,1:T(8,128)(2,1)S(1)} %get-tuple-element.1123), channel_id=1, source_target_pairs={{30,0},{0,2},{2,4},{4,6},{6,8},{8,10},{10,12},{12,14},{14,16},{16,... | collective-permute-start | bytes 491528 | tf_op jit(solution)/shard_map/while/body/eval_jaxpr/ppermute | solution.py:17
  866.6 101.6 %collective-permute-start.2 = (f32[160,512]{0,1:T(8,128)}, f32[160,512]{0,1:T(8,128)}, u32[]{:S(2)}, u32[]{:S(2)}) collective-permute-start(f32[160,512]{0,1:T(8,128)} %get-tuple-element.1124), channel_id=1, source_target_pairs={{30,0},{0,2},{2,4},{4,6},{6,8},{8,10},{10,12},{12,14},{14,16},{16,... | collective-permute-start | bytes 983048 | tf_op jit(solution)/shard_map/while/body/eval_jaxpr/ppermute | solution.py:17
  970.2 28.5 %collective-permute-start.1 = (bf16[160,512]{0,1:T(8,128)(2,1)S(1)}, bf16[160,512]{0,1:T(8,128)(2,1)S(1)}, u32[]{:S(2)}, u32[]{:S(2)}) collective-permute-start(bf16[160,512]{0,1:T(8,128)(2,1)S(1)} %get-tuple-element.1123), channel_id=1, source_target_pairs={{30,0},{0,2},{2,4},{4,6},{6,8},{8,10},{10,12},{12,14},{14,16},{16,... | collective-permute-start | bytes 491528 | tf_op jit(solution)/shard_map/while/body/eval_jaxpr/ppermute | solution.py:17
  978.2 42.0 %collective-permute-start.2 = (f32[160,512]{0,1:T(8,128)}, f32[160,512]{0,1:T(8,128)}, u32[]{:S(2)}, u32[]{:S(2)}) collective-permute-start(f32[160,512]{0,1:T(8,128)} %get-tuple-element.1124), channel_id=1, source_target_pairs={{30,0},{0,2},{2,4},{4,6},{6,8},{8,10},{10,12},{12,14},{14,16},{16,... | collective-permute-start | bytes 983048 | tf_op jit(solution)/shard_map/while/body/eval_jaxpr/ppermute | solution.py:17
  1022.1 42.0 %collective-permute-start.1 = (bf16[160,512]{0,1:T(8,128)(2,1)S(1)}, bf16[160,512]{0,1:T(8,128)(2,1)S(1)}, u32[]{:S(2)}, u32[]{:S(2)}) collective-permute-start(bf16[160,512]{0,1:T(8,128)(2,1)S(1)} %get-tuple-element.1123), channel_id=1, source_target_pairs={{30,0},{0,2},{2,4},{4,6},{6,8},{8,10},{10,12},{12,14},{14,16},{16,... | collective-permute-start | bytes 491528 | tf_op jit(solution)/shard_map/while/body/eval_jaxpr/ppermute | solution.py:17
  1024.0 51.4 %collective-permute-start.2 = (f32[160,512]{0,1:T(8,128)}, f32[160,512]{0,1:T(8,128)}, u32[]{:S(2)}, u32[]{:S(2)}) collective-permute-start(f32[160,512]{0,1:T(8,128)} %get-tuple-element.1124), channel_id=1, source_target_pairs={{30,0},{0,2},{2,4},{4,6},{6,8},{8,10},{10,12},{12,14},{14,16},{16,... | collective-permute-start | bytes 983048 | tf_op jit(solution)/shard_map/while/body/eval_jaxpr/ppermute | solution.py:17
  1077.3 53.7 %collective-permute-start.1 = (bf16[160,512]{0,1:T(8,128)(2,1)S(1)}, bf16[160,512]{0,1:T(8,128)(2,1)S(1)}, u32[]{:S(2)}, u32[]{:S(2)}) collective-permute-start(bf16[160,512]{0,1:T(8,128)(2,1)S(1)} %get-tuple-element.1123), channel_id=1, source_target_pairs={{30,0},{0,2},{2,4},{4,6},{6,8},{8,10},{10,12},{12,14},{14,16},{16,... | collective-permute-start | bytes 491528 | tf_op jit(solution)/shard_map/while/body/eval_jaxpr/ppermute | solution.py:17
  1079.2 67.3 %collective-permute-start.2 = (f32[160,512]{0,1:T(8,128)}, f32[160,512]{0,1:T(8,128)}, u32[]{:S(2)}, u32[]{:S(2)}) collective-permute-start(f32[160,512]{0,1:T(8,128)} %get-tuple-element.1124), channel_id=1, source_target_pairs={{30,0},{0,2},{2,4},{4,6},{6,8},{8,10},{10,12},{12,14},{14,16},{16,... | collective-permute-start | bytes 983048 | tf_op jit(solution)/shard_map/while/body/eval_jaxpr/ppermute | solution.py:17
  1148.5 15.6 collective-permute-start.1
  1150.4 25.1 %collective-permute-start.2 = (f32[160,512]{0,1:T(8,128)}, f32[160,512]{0,1:T(8,128)}, u32[]{:S(2)}, u32[]{:S(2)}) collective-permute-start(f32[160,512]{0,1:T(8,128)} %get-tuple-element.1124), channel_id=1, source_target_pairs={{30,0},{0,2},{2,4},{4,6},{6,8},{8,10},{10,12},{12,14},{14,16},{16,... | collective-permute-start | bytes 983048 | tf_op jit(solution)/shard_map/while/body/eval_jaxpr/ppermute | solution.py:17
  1177.4 53.3 %collective-permute-start.1 = (bf16[160,512]{0,1:T(8,128)(2,1)S(1)}, bf16[160,512]{0,1:T(8,128)(2,1)S(1)}, u32[]{:S(2)}, u32[]{:S(2)}) collective-permute-start(bf16[160,512]{0,1:T(8,128)(2,1)S(1)} %get-tuple-element.1123), channel_id=1, source_target_pairs={{30,0},{0,2},{2,4},{4,6},{6,8},{8,10},{10,12},{12,14},{14,16},{16,... | collective-permute-start | bytes 491528 | tf_op jit(solution)/shard_map/while/body/eval_jaxpr/ppermute | solution.py:17
  1179.3 68.4 %collective-permute-start.2 = (f32[160,512]{0,1:T(8,128)}, f32[160,512]{0,1:T(8,128)}, u32[]{:S(2)}, u32[]{:S(2)}) collective-permute-start(f32[160,512]{0,1:T(8,128)} %get-tuple-element.1124), channel_id=1, source_target_pairs={{30,0},{0,2},{2,4},{4,6},{6,8},{8,10},{10,12},{12,14},{14,16},{16,... | collective-permute-start | bytes 983048 | tf_op jit(solution)/shard_map/while/body/eval_jaxpr/ppermute | solution.py:17
  1249.6 75.9 %collective-permute-start.1 = (bf16[160,512]{0,1:T(8,128)(2,1)S(1)}, bf16[160,512]{0,1:T(8,128)(2,1)S(1)}, u32[]{:S(2)}, u32[]{:S(2)}) collective-permute-start(bf16[160,512]{0,1:T(8,128)(2,1)S(1)} %get-tuple-element.1123), channel_id=1, source_target_pairs={{30,0},{0,2},{2,4},{4,6},{6,8},{8,10},{10,12},{12,14},{14,16},{16,... | collective-permute-start | bytes 491528 | tf_op jit(solution)/shard_map/while/body/eval_jaxpr/ppermute | solution.py:17
  1251.5 89.4 %collective-permute-start.2 = (f32[160,512]{0,1:T(8,128)}, f32[160,512]{0,1:T(8,128)}, u32[]{:S(2)}, u32[]{:S(2)}) collective-permute-start(f32[160,512]{0,1:T(8,128)} %get-tuple-element.1124), channel_id=1, source_target_pairs={{30,0},{0,2},{2,4},{4,6},{6,8},{8,10},{10,12},{12,14},{14,16},{16,... | collective-permute-start | bytes 983048 | tf_op jit(solution)/shard_map/while/body/eval_jaxpr/ppermute | solution.py:17
  1342.8 158.9 %collective-permute-start.1 = (bf16[160,512]{0,1:T(8,128)(2,1)S(1)}, bf16[160,512]{0,1:T(8,128)(2,1)S(1)}, u32[]{:S(2)}, u32[]{:S(2)}) collective-permute-start(bf16[160,512]{0,1:T(8,128)(2,1)S(1)} %get-tuple-element.1123), channel_id=1, source_target_pairs={{30,0},{0,2},{2,4},{4,6},{6,8},{8,10},{10,12},{12,14},{14,16},{16,... | collective-permute-start | bytes 491528 | tf_op jit(solution)/shard_map/while/body/eval_jaxpr/ppermute | solution.py:17
  1480.3 59.3 %collective-permute-start.2 = (f32[160,512]{0,1:T(8,128)}, f32[160,512]{0,1:T(8,128)}, u32[]{:S(2)}, u32[]{:S(2)}) collective-permute-start(f32[160,512]{0,1:T(8,128)} %get-tuple-element.1124), channel_id=1, source_target_pairs={{30,0},{0,2},{2,4},{4,6},{6,8},{8,10},{10,12},{12,14},{14,16},{16,... | collective-permute-start | bytes 983048 | tf_op jit(solution)/shard_map/while/body/eval_jaxpr/ppermute | solution.py:17
  1541.5 19.8 %collective-permute-start.1 = (bf16[160,512]{0,1:T(8,128)(2,1)S(1)}, bf16[160,512]{0,1:T(8,128)(2,1)S(1)}, u32[]{:S(2)}, u32[]{:S(2)}) collective-permute-start(bf16[160,512]{0,1:T(8,128)(2,1)S(1)} %get-tuple-element.1123), channel_id=1, source_target_pairs={{30,0},{0,2},{2,4},{4,6},{6,8},{8,10},{10,12},{12,14},{14,16},{16,... | collective-permute-start | bytes 491528 | tf_op jit(solution)/shard_map/while/body/eval_jaxpr/ppermute | solution.py:17
  1546.1 31.7 %collective-permute-start.2 = (f32[160,512]{0,1:T(8,128)}, f32[160,512]{0,1:T(8,128)}, u32[]{:S(2)}, u32[]{:S(2)}) collective-permute-start(f32[160,512]{0,1:T(8,128)} %get-tuple-element.1124), channel_id=1, source_target_pairs={{30,0},{0,2},{2,4},{4,6},{6,8},{8,10},{10,12},{12,14},{14,16},{16,... | collective-permute-start | bytes 983048 | tf_op jit(solution)/shard_map/while/body/eval_jaxpr/ppermute | solution.py:17
  1579.7 14.2 collective-permute-start.1
  1581.6 23.6 %collective-permute-start.2 = (f32[160,512]{0,1:T(8,128)}, f32[160,512]{0,1:T(8,128)}, u32[]{:S(2)}, u32[]{:S(2)}) collective-permute-start(f32[160,512]{0,1:T(8,128)} %get-tuple-element.1124), channel_id=1, source_target_pairs={{30,0},{0,2},{2,4},{4,6},{6,8},{8,10},{10,12},{12,14},{14,16},{16,... | collective-permute-start | bytes 983048 | tf_op jit(solution)/shard_map/while/body/eval_jaxpr/ppermute | solution.py:17
  1607.1 64.0 %collective-permute-start.1 = (bf16[160,512]{0,1:T(8,128)(2,1)S(1)}, bf16[160,512]{0,1:T(8,128)(2,1)S(1)}, u32[]{:S(2)}, u32[]{:S(2)}) collective-permute-start(bf16[160,512]{0,1:T(8,128)(2,1)S(1)} %get-tuple-element.1123), channel_id=1, source_target_pairs={{30,0},{0,2},{2,4},{4,6},{6,8},{8,10},{10,12},{12,14},{14,16},{16,... | collective-permute-start | bytes 491528 | tf_op jit(solution)/shard_map/while/body/eval_jaxpr/ppermute | solution.py:17
  1610.6 71.9 %collective-permute-start.2 = (f32[160,512]{0,1:T(8,128)}, f32[160,512]{0,1:T(8,128)}, u32[]{:S(2)}, u32[]{:S(2)}) collective-permute-start(f32[160,512]{0,1:T(8,128)} %get-tuple-element.1124), channel_id=1, source_target_pairs={{30,0},{0,2},{2,4},{4,6},{6,8},{8,10},{10,12},{12,14},{14,16},{16,... | collective-permute-start | bytes 983048 | tf_op jit(solution)/shard_map/while/body/eval_jaxpr/ppermute | solution.py:17
  1684.4 16.5 collective-permute-start.1
  1686.3 28.7 %collective-permute-start.2 = (f32[160,512]{0,1:T(8,128)}, f32[160,512]{0,1:T(8,128)}, u32[]{:S(2)}, u32[]{:S(2)}) collective-permute-start(f32[160,512]{0,1:T(8,128)} %get-tuple-element.1124), channel_id=1, source_target_pairs={{30,0},{0,2},{2,4},{4,6},{6,8},{8,10},{10,12},{12,14},{14,16},{16,... | collective-permute-start | bytes 983048 | tf_op jit(solution)/shard_map/while/body/eval_jaxpr/ppermute | solution.py:17
  1718.1 28.0 %collective-permute-start.3 = (f32[160,512]{1,0:T(8,128)S(1)}, f32[160,512]{1,0:T(8,128)S(1)}, u32[]{:S(2)}, u32[]{:S(2)}) collective-permute-start(f32[160,512]{1,0:T(8,128)S(1)} %copy.400), channel_id=1, source_target_pairs={{30,0},{0,2},{2,4},{4,6},{6,8},{8,10},{10,12},{12,14},{14,16},{16,... | collective-permute-start | bytes 983048 | tf_op jit(solution)/shard_map/ppermute | solution.py:17
  1730.0 6.9 all-to-all-start.1
  (4 other events, 5.5 us)
where the time goes:
time: 1880 us; the launch traced here: 1870 us
  waiting for transfers between devices  1050 us (56%)
  starting transfers between devices  471 us (25%)
  blocking collectives  153 us (8%)
  other arithmetic  71.4 us (4%)
  local copies, waits for them, and re-layouts  56.1 us (3%)
  matrix products  42 us (2%)
  loops' own time  23 us (1%)
    ppermute x46, waiting for transfers between devices, passed_along(): return lax.ppermute(block, axis, route)  1050 us
    ppermute x46, starting transfers between devices, passed_along(): return lax.ppermute(block, axis, route)  454 us
    unnamed x1, blocking collectives  108 us
  transfers between devices with their start and end apart: 48, of which 46 were waited for; matrix products, arithmetic and copies ran while one was open for 4% of the time, Pallas kernels for 0%

commit v1 on v0

v1 whole, which is shorter than its diff:
```python
import functools
import math

import jax
import jax.numpy as jnp
from jax import lax
from jax.experimental import pallas as pl
from jax.experimental.pallas import tpu as pltpu
from jax.sharding import PartitionSpec as P

HD = 128
SOFTCAP = 50.0
SCORE_FACTOR = 1.0 / (math.sqrt(HD) * SOFTCAP)
EXP2_FACTOR = SOFTCAP * math.log2(math.e)
INV_ROOT = 1.0 / math.sqrt(HD)

NX, NZL, NY, NZH, NC = 4, 4, 4, 4, 2
NZ = NZL * NZH
BLOCK = 128
HALF = BLOCK // NC
LANES = 512
PROMPT = 512
BASE = [BLOCK * (yb * (yb + 1) // 2) for yb in range(NY)]
SEEN = BLOCK * (NY * (NY + 1) // 2)
OWN, LEFT, RIGHT, FAR = range(4)
MESH = pl.DeviceIdType.MESH

F32 = jnp.float32
BF16 = jnp.bfloat16


def dot(a, b):
    return jnp.dot(a, b, preferred_element_type=F32)


def dot_rows(a, b):
    return lax.dot_general(a, b, (((1,), (1,)), ((), ())), preferred_element_type=F32)


def dot_first(a, b):
    return lax.dot_general(a, b, (((0,), (0,)), ((), ())), preferred_element_type=F32)


def stack_heads(rows):
    return jnp.concatenate([rows[:, h * HD : (h + 1) * HD] for h in range(4)], axis=0)


def kernel(
    len_ref, q_ref, k_ref, v_ref, g_ref, pp_ref,
    gq_ref, gk_ref, gv_ref, gp_ref,
    qb, gb, kz, vz, ka, va, pz, px, pk, pv,
    ep, wp, dp, er, wr, dr,
    tot, rdot, dqt, acc, send_kv, recv_kv, send_z, recv_z,
    send_p, recv_p, part_p, recv_x, tile_p, recv_t, out_q,
    sem_pz, sem_z, sem_q, sem_g, sem_kv, sem_px, sem_py,
    sem_rs, sem_zr, sem_sp, sem_sx, sem_st, sem_oq, sem_own,
):
    resp, pre, core = (lax.axis_index(a) for a in ("resp", "pre", "head"))
    x, zl = resp // NZL, resp % NZL
    y, zh = pre // NZH, pre % NZH
    z = zh * NZL + zl
    left, right, far = (zh + NZH - 1) % NZH, (zh + 1) % NZH, (zh + 2) % NZH
    place_of = [zh, left, right, far]

    def device(x=x, zl=zl, y=y, zh=zh, core=core):
        return {"resp": x * NZL + zl, "pre": y * NZH + zh, "head": core}

    z_partners = [
        ((zl + a) % NZL, (zh + b) % NZH) for b in range(NZH) for a in range(NZL) if a or b
    ]
    y_partners = [(y + a) % NY for a in range(1, NY)]
    yc_partners = [
        ((y + a) % NY, (core + b) % NC) for a in range(NY) for b in range(NC) if a or b
    ]
    x_partners = [(x + a) % NX for a in range(1, NX)]

    started = []

    def send(src, dst, sems, index, to):
        copy = pltpu.make_async_remote_copy(
            src_ref=src,
            dst_ref=dst,
            send_sem=sems.at[(0, *index)],
            recv_sem=sems.at[(1, *index)],
            device_id=to,
            device_id_type=MESH,
        )
        copy.start()
        started.append(copy)
        return copy

    def local(src, dst, index):
        copy = pltpu.make_async_copy(src, dst, sem_own.at[index])
        copy.start()
        return copy

    barrier = pltpu.get_barrier_semaphore()
    greeted = [device(zl=a, zh=b) for a, b in z_partners]
    greeted += [device(y=a, core=b) for a, b in yc_partners]
    greeted += [device(x=a) for a in x_partners]
    for to in greeted:
        pl.semaphore_signal(barrier, inc=1, device_id=to, device_id_type=MESH)
    pl.semaphore_wait(barrier, len(greeted))

    def cols(start, width):
        return pl.ds(pl.multiple_of(start, HD), width)

    def rows(start, count):
        return pl.ds(pl.multiple_of(start, 16), count)

    from_left_k = send(k_ref, kz.at[zh], sem_z, (0,), device(zh=right))
    from_right_v = send(v_ref, vz.at[zh], sem_z, (1,), device(zh=left))
    from_left_v = send(v_ref, vz.at[zh], sem_z, (2,), device(zh=right))
    from_right_k = send(k_ref, kz.at[zh], sem_z, (3,), device(zh=left))

    pieces = [
        send(
            pp_ref,
            pz.at[pl.ds(pl.multiple_of(z * 8, 8), 8)],
            sem_pz,
            (i,),
            device(zl=a, zh=b),
        )
        for i, (a, b) in enumerate(z_partners)
    ]
    pz[pl.ds(pl.multiple_of(z * 8, 8), 8), :] = pp_ref[...]

    queries_in = [
        send(q_ref.at[:, cols(a * LANES, LANES)], qb.at[y], sem_q, (i,), device(y=a))
        for i, a in enumerate(y_partners)
    ]
    own = [local(q_ref.at[:, cols(y * LANES, LANES)], qb.at[y], 0)]

    def spread(step, key_ref, value_ref):
        at = pl.ds(pl.multiple_of(y * BLOCK, BLOCK), BLOCK)
        copies = []
        for i, a in enumerate(y_partners):
            group = cols((a // 2) * HD, HD)
            to = device(y=a)
            zs = place_of[step]
            copies.append(send(key_ref.at[:, group], ka.at[zs, at], sem_kv, (step, 0, i), to))
            copies.append(send(value_ref.at[:, group], va.at[zs, at], sem_kv, (step, 1, i), to))
        group = cols((y // 2) * HD, HD)
        copies_own = [
            local(key_ref.at[:, group], ka.at[place_of[step], at], 2 + 2 * step),
            local(value_ref.at[:, group], va.at[place_of[step], at], 3 + 2 * step),
        ]
        return copies, copies_own

    block_in = [spread(OWN, k_ref, v_ref), None, None, None]
    grads_in = [
        send(
            g_ref.at[:, cols(b * (NY * LANES) + a * LANES, LANES)],
            gb.at[y, rows(core * HALF, HALF)],
            sem_g,
            (i,),
            device(y=a, core=b),
        )
        for i, (a, b) in enumerate(yc_partners)
    ]
    own.append(
        local(
            g_ref.at[:, cols(core * (NY * LANES) + y * LANES, LANES)],
            gb.at[y, rows(core * HALF, HALF)],
            1,
        )
    )

    for copy in pieces:
        copy.wait_recv()
    mine_x = pl.ds(pl.multiple_of(x * 32, 32), 32)
    for t in range(4):
        for k in range(2):
            piece = pz[pl.ds(t * 2 + k, NZ, stride=8), :].astype(BF16)
            px[t, pl.ds(pl.multiple_of(x * 32 + k * 16, 16), 16), :] = piece
    prompt_x = [
        send(px.at[:, mine_x], px.at[:, mine_x], sem_px, (i,), device(x=a))
        for i, a in enumerate(x_partners)
    ]

    from_left_k.wait_recv()
    far_k = send(kz.at[left], kz.at[left], sem_z, (4,), device(zh=right))
    from_right_v.wait_recv()
    far_v = send(vz.at[right], vz.at[right], sem_z, (5,), device(zh=left))

    for copy in prompt_x:
        copy.wait_recv()
    mine_y = pl.ds(pl.multiple_of(y * BLOCK, BLOCK), BLOCK)
    prompt_y = []
    for i, a in enumerate(y_partners):
        prompt_y.append(send(px.at[a // 2], pk.at[mine_y], sem_py, (0, i), device(y=a)))
        prompt_y.append(send(px.at[2 + a // 2], pv.at[mine_y], sem_py, (1, i), device(y=a)))
    own_prompt = [
        local(px.at[y // 2], pk.at[mine_y], 10),
        local(px.at[2 + y // 2], pv.at[mine_y], 11),
    ]

    for copy in queries_in + grads_in:
        copy.wait_recv()
    for copy in own:
        copy.wait()
    length = len_ref[0]
    for yb in range(NY):
        pos = lax.broadcasted_iota(jnp.int32, (BLOCK, LANES), 0) + (yb * NZH + zh) * BLOCK
        gb[yb] = jnp.where(pos < length, gb[yb].astype(F32), 0.0).astype(BF16)
        tot[yb] = jnp.zeros((8, LANES), F32)
        rdot[yb] = jnp.zeros((8, LANES), F32)
        dqt[yb] = jnp.zeros((HD, LANES), F32)

    key_at = lax.broadcasted_iota(jnp.int32, (BLOCK, LANES), 0)
    query_at = lax.broadcasted_iota(jnp.int32, (BLOCK, LANES), 1) % BLOCK
    gap = key_at - query_at

    def first_pass(yb, keys, values, count, e_ref, w_ref, d_ref, base, limit):
        queries, grads = stack_heads(qb[yb]), stack_heads(gb[yb])
        total, row_dot = tot[yb], rdot[yb]
        for c in range(count):
            at = pl.ds(c * BLOCK, BLOCK)
            score = dot_rows(keys[at, :], queries)
            grad_prob = dot_rows(values[at, :], grads)
            tangent = jnp.tanh(score * SCORE_FACTOR)
            weight = jnp.exp2(tangent * EXP2_FACTOR)
            if limit is not None and c == count - 1:
                weight = jnp.where(gap <= limit, weight, 0.0)
            slope = weight * (1.0 - tangent * tangent)
            total = total + weight.reshape(BLOCK // 8, 8, LANES).sum(0)
            row_dot = row_dot + (weight * grad_prob).reshape(BLOCK // 8, 8, LANES).sum(0)
            to = pl.ds(base + c * BLOCK, BLOCK)
            e_ref[to, :] = weight.astype(BF16)
            w_ref[to, :] = slope.astype(BF16)
            d_ref[to, :] = grad_prob.astype(BF16)
        tot[yb] = total
        rdot[yb] = row_dot

    def response_first(step):
        zs = place_of[step]
        limit = (zh - zs) * BLOCK
        copies, copies_own = block_in[step]
        for copy in copies:
            copy.wait_recv()
        for copy in copies_own:
            copy.wait()
        for yb in range(NY):
            first_pass(
                yb, ka.at[zs], va.at[zs], yb + 1,
                er.at[step], wr.at[step], dr.at[step], BASE[yb], limit,
            )

    response_first(OWN)
    from_left_v.wait_recv()
    block_in[LEFT] = spread(LEFT, kz.at[left], vz.at[left])
    from_right_k.wait_recv()
    block_in[RIGHT] = spread(RIGHT, kz.at[right], vz.at[right])

    for copy in prompt_y:
        copy.wait_recv()
    for copy in own_prompt:
        copy.wait()
    for yb in range(NY):
        first_pass(yb, pk, pv, PROMPT // BLOCK, ep.at[yb], wp.at[yb], dp.at[yb], 0, None)

    response_first(LEFT)
    far_k.wait_recv()
    far_v.wait_recv()
    block_in[FAR] = spread(FAR, kz.at[far], vz.at[far])
    response_first(RIGHT)
    response_first(FAR)

    for yb in range(NY):
        total = jnp.sum(tot[yb], axis=0, keepdims=True)
        row_dot = jnp.sum(rdot[yb], axis=0, keepdims=True)
        inverse = 1.0 / total
        tot[yb] = jnp.broadcast_to(inverse, (8, LANES))
        rdot[yb] = jnp.broadcast_to(row_dot * inverse, (8, LANES))

    def second_pass(yb, keys, count, e_ref, w_ref, d_ref, base, fresh):
        queries, grads = stack_heads(qb[yb]), stack_heads(gb[yb])
        inverse = tot[yb, 0:1, :]
        inverse_root = inverse * INV_ROOT
        row_dot = rdot[yb, 0:1, :]
        query_grad = dqt[yb]
        for c in range(count):
            at = pl.ds(base + c * BLOCK, BLOCK)
            to = pl.ds(c * BLOCK, BLOCK)
            prob = (e_ref[at, :].astype(F32) * inverse).astype(BF16)
            grad_score = (
                (w_ref[at, :].astype(F32) * inverse_root) * (d_ref[at, :].astype(F32) - row_dot)
            ).astype(BF16)
            key_grad = dot(grad_score, queries)
            value_grad = dot(prob, grads)
            query_grad = query_grad + dot_first(keys[to, :], grad_score)
            if fresh(c):
                acc[0, to, :] = key_grad
                acc[1, to, :] = value_grad
            else:
                acc[0, to, :] += key_grad
                acc[1, to, :] += value_grad
        dqt[yb] = query_grad

    partials = [None] * 4

    def response_second(step):
        for yb in range(NY):
            second_pass(
                yb, ka.at[place_of[step]], yb + 1,
                er.at[step], wr.at[step], dr.at[step], BASE[yb], lambda c, yb=yb: c == yb,
            )
        send_kv[step] = acc[...].astype(BF16)
        partials[step] = [
            send(
                send_kv.at[step, :, rows(a * BLOCK + b * HALF, HALF)],
                recv_kv.at[step, y * NC + core],
                sem_rs,
                (step, i),
                device(y=a, core=b),
            )
            for i, (a, b) in enumerate(yc_partners)
        ]
        recv_kv[step, y * NC + core] = send_kv[step, :, rows(y * BLOCK + core * HALF, HALF), :]

    def summed(step, which):
        groups = []
        for c in range(NC):
            for g in range(2):
                first = recv_kv[step, (2 * g) * NC + c, which].astype(F32)
                second = recv_kv[step, (2 * g + 1) * NC + c, which].astype(F32)
                groups.append(first + second)
        return jnp.concatenate(groups, axis=1)

    def collect(step):
        for copy in partials[step]:
            copy.wait_recv()

    response_second(FAR)
    response_second(LEFT)
    collect(FAR)
    for which in range(2):
        send_z[FAR, which] = summed(FAR, which).astype(BF16)
    far_key = send(send_z.at[FAR, 0], recv_z.at[0], sem_zr, (0,), device(zh=right))
    far_value = send(send_z.at[FAR, 1], recv_z.at[1], sem_zr, (1,), device(zh=left))

    response_second(RIGHT)
    collect(LEFT)
    send_z[LEFT, 0] = summed(LEFT, 0).astype(BF16)
    key_right = send(send_z.at[LEFT, 0], recv_z.at[4], sem_zr, (4,), device(zh=left))

    for yb in range(NY):
        second_pass(
            yb, pk, PROMPT // BLOCK, ep.at[yb], wp.at[yb], dp.at[yb], 0, lambda c, yb=yb: yb == 0
        )
    send_p[...] = acc[...].astype(BF16)
    prompt_back = [
        send(
            send_p.at[:, pl.ds(pl.multiple_of(a * BLOCK, BLOCK), BLOCK)],
            recv_p.at[y],
            sem_sp,
            (i,),
            device(y=a),
        )
        for i, a in enumerate(y_partners)
    ]
    recv_p[y] = send_p[:, pl.ds(pl.multiple_of(y * BLOCK, BLOCK), BLOCK), :]

    collect(RIGHT)
    send_z[RIGHT, 1] = summed(RIGHT, 1).astype(BF16)
    value_left = send(send_z.at[RIGHT, 1], recv_z.at[3], sem_zr, (3,), device(zh=right))
    far_key.wait_recv()
    send_z[RIGHT, 0] = (summed(RIGHT, 0) + recv_z[0].astype(F32)).astype(BF16)
    key_left = send(send_z.at[RIGHT, 0], recv_z.at[2], sem_zr, (2,), device(zh=right))
    far_value.wait_recv()
    send_z[LEFT, 1] = (summed(LEFT, 1) + recv_z[1].astype(F32)).astype(BF16)
    value_right = send(send_z.at[LEFT, 1], recv_z.at[5], sem_zr, (5,), device(zh=left))

    response_second(OWN)

    for yb in range(NY):
        for h in range(4):
            at = pl.ds(h * HD, HD)
            out_q[yb, :, at] = dqt[yb, :, at].T.astype(BF16)
    mine = cols(core * (NY * LANES) + y * LANES, LANES)
    query_back = [
        send(
            out_q.at[a, rows(b * HALF, HALF)],
            gq_ref.at[:, mine],
            sem_oq,
            (i,),
            device(y=a, core=b),
        )
        for i, (a, b) in enumerate(yc_partners)
    ]
    own_back = local(out_q.at[y, rows(core * HALF, HALF)], gq_ref.at[:, mine], 12)

    for copy in prompt_back:
        copy.wait_recv()
    for which in range(2):
        for g in range(2):
            part_p[2 * which + g] = recv_p[2 * g, which].astype(F32) + recv_p[
                2 * g + 1, which
            ].astype(F32)
    prompt_x_back = [
        send(
            part_p.at[:, pl.ds(pl.multiple_of(a * 32, 32), 32)],
            recv_x.at[i],
            sem_sx,
            (i,),
            device(x=a),
        )
        for i, a in enumerate(x_partners)
    ]
    for copy in prompt_x_back:
        copy.wait_recv()
    for t in range(4):
        part = part_p[t, mine_x, :]
        for i in range(NX - 1):
            part = part + recv_x[i, t]
        for k in range(2):
            tile_p[pl.ds(t * 2 + k, NZ, stride=8), :] = part[k * 16 : (k + 1) * 16]
    tiles_back = [
        send(
            tile_p.at[pl.ds(pl.multiple_of((b * NZL + a) * 8, 8), 8)],
            recv_t.at[i],
            sem_st,
            (i,),
            device(zl=a, zh=b),
        )
        for i, (a, b) in enumerate(z_partners)
    ]

    collect(OWN)
    key_left.wait_recv()
    key_right.wait_recv()
    gk_ref[...] = (summed(OWN, 0) + recv_z[2].astype(F32) + recv_z[4].astype(F32)).astype(BF16)
    value_left.wait_recv()
    value_right.wait_recv()
    gv_ref[...] = (summed(OWN, 1) + recv_z[3].astype(F32) + recv_z[5].astype(F32)).astype(BF16)

    for copy in tiles_back:
        copy.wait_recv()
    tile = tile_p[pl.ds(pl.multiple_of(z * 8, 8), 8), :]
    for i in range(NZ - 1):
        tile = tile + recv_t[i]
    gp_ref[...] = tile

    for copy in query_back:
        copy.wait_recv()
    own_back.wait()
    for copy in started:
        copy.wait_send()


def shards(queries, keys, values, prefix_keys, prefix_values, grad_out, lengths):
    def by_group(prompt_rows):
        return prompt_rows.reshape(2, 2, HD).transpose(1, 0, 2).reshape(4, HD)

    prompt = jnp.concatenate([by_group(prefix_keys), by_group(prefix_values)], axis=0).astype(F32)
    vmem = pl.BlockSpec(memory_space=pltpu.VMEM)
    anywhere = pl.BlockSpec(memory_space=pl.ANY)
    smem = pl.BlockSpec(memory_space=pltpu.SMEM)

    def sems(*dims):
        return pltpu.SemaphoreType.DMA((2, *dims))

    grad_queries, grad_keys, grad_values, grad_prompt = pl.pallas_call(
        kernel,
        out_shape=(
            jax.ShapeDtypeStruct((HALF, NC * NY * LANES), BF16),
            jax.ShapeDtypeStruct((HALF, 4 * HD), BF16),
            jax.ShapeDtypeStruct((HALF, 4 * HD), BF16),
            jax.ShapeDtypeStruct((8, HD), F32),
        ),
        in_specs=[smem, anywhere, anywhere, anywhere, anywhere, vmem],
        out_specs=(anywhere, vmem, vmem, vmem),
        scratch_shapes=[
            pltpu.VMEM((NY, BLOCK, LANES), BF16),
            pltpu.VMEM((NY, BLOCK, LANES), BF16),
            pltpu.VMEM((NZH, BLOCK, 2 * HD), BF16),
            pltpu.VMEM((NZH, BLOCK, 2 * HD), BF16),
            pltpu.VMEM((NZH, NY * BLOCK, HD), BF16),
            pltpu.VMEM((NZH, NY * BLOCK, HD), BF16),
            pltpu.VMEM((NZ * 8, HD), F32),
            pltpu.VMEM((4, NX * 32, HD), BF16),
            pltpu.VMEM((PROMPT, HD), BF16),
            pltpu.VMEM((PROMPT, HD), BF16),
            pltpu.VMEM((NY, PROMPT, LANES), BF16),
            pltpu.VMEM((NY, PROMPT, LANES), BF16),
            pltpu.VMEM((NY, PROMPT, LANES), BF16),
            pltpu.VMEM((NZH, SEEN, LANES), BF16),
            pltpu.VMEM((NZH, SEEN, LANES), BF16),
            pltpu.VMEM((NZH, SEEN, LANES), BF16),
            pltpu.VMEM((NY, 8, LANES), F32),
            pltpu.VMEM((NY, 8, LANES), F32),
            pltpu.VMEM((NY, HD, LANES), F32),
            pltpu.VMEM((2, NY * BLOCK, HD), F32),
            pltpu.VMEM((NZH, 2, NY * BLOCK, HD), BF16),
            pltpu.VMEM((NZH, NY * NC, 2, HALF, HD), BF16),
            pltpu.VMEM((NZH, 2, HALF, 4 * HD), BF16),
            pltpu.VMEM((6, HALF, 4 * HD), BF16),
            pltpu.VMEM((2, PROMPT, HD), BF16),
            pltpu.VMEM((NY, 2, BLOCK, HD), BF16),
            pltpu.VMEM((4, NX * 32, HD), F32),
            pltpu.VMEM((NX - 1, 4, 32, HD), F32),
            pltpu.VMEM((NZ * 8, HD), F32),
            pltpu.VMEM((NZ - 1, 8, HD), F32),
            pltpu.VMEM((NY, BLOCK, LANES), BF16),
            sems(NZ - 1),
            sems(6),
            sems(NY - 1),
            sems(NY * NC - 1),
            sems(NZH, 2, NY - 1),
            sems(NX - 1),
            sems(2, NY - 1),
            sems(NZH, NY * NC - 1),
            sems(6),
            sems(NY - 1),
            sems(NX - 1),
            sems(NZ - 1),
            sems(NY * NC - 1),
            pltpu.SemaphoreType.DMA((13,)),
        ],
        compiler_params=pltpu.CompilerParams(
            collective_id=0, has_side_effects=True, vmem_limit_bytes=48 * 2**20
        ),
        name="attention_grads",
    )(lengths, queries[0], keys[0], values[0], grad_out[0], prompt)

    def rows_of(block):
        return block.reshape(2, 2, HD).transpose(1, 0, 2).reshape(2, 2 * HD).astype(BF16)

    return (
        grad_queries[None],
        grad_keys[None],
        grad_values[None],
        rows_of(grad_prompt[:4]),
        rows_of(grad_prompt[4:]),
    )


def solution(mesh):
    in_specs = (
        P("resp", "pre", "head"),
        P("resp", "pre", "head"),
        P("resp", "pre", "head"),
        P(("resp", "pre"), "head"),
        P(("resp", "pre"), "head"),
        P("resp", ("pre", "head"), None),
        P("resp"),
    )
    out_specs = (
        P("resp", ("pre", "head"), None),
        P("resp", ("pre", "head"), None),
        P("resp", ("pre", "head"), None),
        P(("resp", "pre"), "head"),
        P(("resp", "pre"), "head"),
    )
    return jax.shard_map(shards, mesh=mesh, in_specs=in_specs, out_specs=out_specs, check_vma=False)
```

time: 1880 us -> 99.2 us (0.05)
  waiting for transfers between devices: 1050 us -> 0 us
  starting transfers between devices: 471 us -> 0 us
  blocking collectives: 153 us -> 0 us
  Pallas kernels: 0 us -> 90.2 us
  other arithmetic: 71.4 us -> 0.01 us
  local copies, waits for them, and re-layouts: 56.1 us -> 7.06 us
  matrix products: 42 us -> 0 us
  loops' own time: 23 us -> 0 us
    ppermute x46 -> x0, waiting for transfers between devices: 1050 us -> none  [passed_along(): return lax.ppermute(block, axis, route)]
    ppermute x46 -> x0, starting transfers between devices: 454 us -> none  [passed_along(): return lax.ppermute(block, axis, route)]
    unnamed x1 -> x0, blocking collectives: 108 us -> none
    pallas_call x0 -> x1, Pallas kernels: none -> 90.2 us  [shards(): pl.pallas_call(kernel, out_shape=(jax.ShapeDtypeStruct((HALF, NC * NY * L...]
    dot_general x118 -> x0, matrix products: 42 us -> none  [the longest x33 11.1 us: tangents(): jnp.einsum('igkd,jgd->gkij', query_heads, key_part, preferred_element_typ...]
    add x64 -> x0, other arithmetic: 36.2 us -> none  [the longest x15 28.3 us: grad_loop(): return (block_rows, travel + block_term, grad_query)]
    all_gather x1 -> x0, blocking collectives: 31.1 us -> none  [shards(): prompt_rows = lax.all_gather(prompt_own, 'resp', axis=0, tiled=True)]
    unnamed x5 -> x0, other arithmetic: 28.7 us -> none
  transfers between devices with their start and end apart: 48 -> 0, of which waited for: 46 -> 0; matrix products, arithmetic and copies ran while one was open for 4% -> 0% of each run, Pallas kernels for 0% -> 0%
where the time goes in v1:
time: 99.2 us; the launch traced here: 98.6 us
  Pallas kernels  90.2 us (91%)
  local copies, waits for them, and re-layouts  7.06 us (7%)
  between operations  1.33 us (1%)
    pallas_call x1, Pallas kernels, shards(): pl.pallas_call(kernel, out_shape=(jax.ShapeDtypeStruct((HALF, NC * NY * L...  90.2 us
    unnamed x15, local copies, waits for them, and re-layouts  6.49 us

profile of v1, /device:TPU:1, one launch (start us, length us, event | category | flops | bytes accessed | tf_op | source)
XLA Modules:
  0.0 98.6 jit_solution(9379988049173120796)
XLA Ops:
  0.6 0.0 copy-start.5
  0.6 0.0 copy-start.4
  0.7 0.7 copy-done.5
  1.3 0.0 copy-done.4
  2.0 0.0 copy-start
  2.0 1.0 %copy-done = bf16[1,128,2048]{2,1,0:T(8,128)(2,1)S(1)} copy-done((bf16[1,128,2048]{2,1,0:T(8,128)(2,1)S(1)}, bf16[1,128,2048]{2,1,0:T(8,128)(2,1)}, u32[]{:S(2)}) %copy-start) | copy-done | bytes 524312
  3.0 0.0 copy-start.1
  3.0 1.0 %copy-done.1 = bf16[1,64,4096]{2,1,0:T(8,128)(2,1)S(1)} copy-done((bf16[1,64,4096]{2,1,0:T(8,128)(2,1)S(1)}, bf16[1,64,4096]{2,1,0:T(8,128)(2,1)}, u32[]{:S(2)}) %copy-start.1) | copy-done | bytes 524312
  4.1 0.0 copy-start.2
  4.1 0.8 copy-done.2
  4.9 0.0 copy-start.3
  4.9 0.8 copy-done.3
  5.8 90.2 %attention_grads.1 = (bf16[64,4096]{1,0:T(8,128)(2,1)S(1)}, bf16[64,512]{1,0:T(8,128)(2,1)S(1)}, bf16[64,512]{1,0:T(8,128)(2,1)S(1)}, f32[8,128]{1,0:T(8,128)S(1)}) custom-call(s32[1]{0:T(128)S(6)} %copy.19.len_ref, bf16[128,2048]{1,0:T(8,128)(2,1)S(1)} %bitcast.27, bf16[128,256]{1,0:T(8,128)(2,1)S(1)} %bitcast.30, bf16[128,256]{1,0:T(8,128)(2,1)S(1)} %bitcast.31, ...), custom_call_target="tpu_custom_call" | custom-call | tf_op jit(solution)/shard_map/attention_grads/pallas_call | solution.py:463
  96.0 0.6 fusion
  96.5 0.8 copy.20
  97.3 0.6 copy.21
  98.0 0.6 copy.22
  (2 shorter events, 0.0 us)
Async XLA Ops:
  0.6 0.7 copy-start.5
  0.6 0.7 copy-start.4
  2.0 1.0 %copy-start = (bf16[1,128,2048]{2,1,0:T(8,128)(2,1)S(1)}, bf16[1,128,2048]{2,1,0:T(8,128)(2,1)}, u32[]{:S(2)}) copy-start(bf16[1,128,2048]{2,1,0:T(8,128)(2,1)} %param.7) | copy-start | bytes 1572868
  3.0 1.0 %copy-start.1 = (bf16[1,64,4096]{2,1,0:T(8,128)(2,1)S(1)}, bf16[1,64,4096]{2,1,0:T(8,128)(2,1)}, u32[]{:S(2)}) copy-start(bf16[1,64,4096]{2,1,0:T(8,128)(2,1)} %param.12) | copy-start | bytes 1572868
  4.1 0.8 copy-start.2
  4.9 0.8 copy-start.3

commit v2 on v1

v2 whole, which is shorter than its diff:
```python
import functools
import math

import jax
import jax.numpy as jnp
from jax import lax
from jax.experimental import pallas as pl
from jax.experimental.pallas import tpu as pltpu
from jax.sharding import PartitionSpec as P

HD = 128
SOFTCAP = 50.0
SCORE_FACTOR = 1.0 / (math.sqrt(HD) * SOFTCAP)
EXP2_FACTOR = SOFTCAP * math.log2(math.e)
INV_ROOT = 1.0 / math.sqrt(HD)

NX, NZL, NY, NZH, NC = 4, 4, 4, 4, 2
NZ = NZL * NZH
BLOCK = 128
HALF = BLOCK // NC
LANES = 512
PROMPT = 512
VMEM_BYTES = 62 * 2**20
BASE = [BLOCK * (yb * (yb + 1) // 2) for yb in range(NY)]
SEEN = BLOCK * (NY * (NY + 1) // 2)
OWN, LEFT, RIGHT, FAR = range(4)
MESH = pl.DeviceIdType.MESH

F32 = jnp.float32
BF16 = jnp.bfloat16


def dot(a, b):
    return jnp.dot(a, b, preferred_element_type=F32)


def dot_rows(a, b):
    return lax.dot_general(a, b, (((1,), (1,)), ((), ())), preferred_element_type=F32)


def dot_first(a, b):
    return lax.dot_general(a, b, (((0,), (0,)), ((), ())), preferred_element_type=F32)


def stack_heads(rows):
    return jnp.concatenate([rows[:, h * HD : (h + 1) * HD] for h in range(4)], axis=0)


def kernel(
    len_ref, q_ref, k_ref, v_ref, g_ref, pk_ref, pv_ref,
    gq_ref, gk_ref, gv_ref, gpk_ref, gpv_ref,
    qb, gb, kvz, kva, pz, px, pkv,
    ep, wp, dp, er, wr, dr,
    tot, rdot, dqt, acc, other, send_kv, recv_kv, send_z, recv_z,
    send_p, part_p, recv_x, tile_p, recv_t, out_q,
    sem_pz, sem_z, sem_qs, sem_qr, sem_g, sem_kvs, sem_kvr, sem_ex, sem_px, sem_pys, sem_pyr,
    sem_rx, sem_rs, sem_zr, sem_sps, sem_spr, sem_sx, sem_st, sem_oq, sem_own,
):
    resp, pre, core = (lax.axis_index(a) for a in ("resp", "pre", "head"))
    x, zl = resp // NZL, resp % NZL
    y, zh = pre // NZH, pre % NZH
    z = zh * NZL + zl
    left, right, far = (zh + NZH - 1) % NZH, (zh + 1) % NZH, (zh + 2) % NZH
    place_of = [zh, left, right, far]

    def device(x=x, zl=zl, y=y, zh=zh, core=core):
        return {"resp": x * NZL + zl, "pre": y * NZH + zh, "head": core}

    z_partners = [
        ((zl + a) % NZL, (zh + b) % NZH) for b in range(NZH) for a in range(NZL) if a or b
    ]
    yc_partners = [
        ((y + a) % NY, (core + b) % NC) for a in range(NY) for b in range(NC) if a or b
    ]
    x_partners = [(x + a) % NX for a in range(1, NX)]

    started = []

    def send(src, dst, sems, index, to):
        copy = pltpu.make_async_remote_copy(
            src_ref=src,
            dst_ref=dst,
            send_sem=sems.at[(0, *index)],
            recv_sem=sems.at[(1, *index)],
            device_id=to,
            device_id_type=MESH,
        )
        copy.start()
        started.append(copy)
        return copy

    conditional = []

    def deliver(src, dst, send_sem, recv_sem, to, here):
        copy = pltpu.make_async_remote_copy(
            src_ref=src,
            dst_ref=dst,
            send_sem=send_sem,
            recv_sem=recv_sem,
            device_id=to,
            device_id_type=MESH,
        )

        @pl.when(here)
        def _():
            pltpu.make_async_copy(src, dst, recv_sem).start()

        @pl.when(jnp.logical_not(here))
        def _():
            copy.start()

        conditional.append((copy, here))

    def delivered(dst, recv_sem):
        pltpu.make_async_copy(dst, dst, recv_sem).wait()

    def local(src, dst, index):
        copy = pltpu.make_async_copy(src, dst, sem_own.at[index])
        copy.start()
        return copy

    def cols(start, width):
        return pl.ds(pl.multiple_of(start, HD), width)

    def rows(start, count):
        return pl.ds(pl.multiple_of(start, 16), count)

    packed = [
        local(ref.at[:, pl.ds(g * HD, HD)], kvz.at[zh, g, which], 2 + 2 * g + which)
        for g in range(2)
        for which, ref in enumerate((k_ref, v_ref))
    ]
    mine_g = cols(y * (NC * LANES) + core * LANES, LANES)
    own_grads = local(g_ref.at[:, mine_g], gb.at[y, rows(core * HALF, HALF)], 1)
    mine_z = pl.ds(pl.multiple_of(z * 8, 8), 8)
    pz[mine_z, :] = jnp.concatenate(
        [
            ref[:, g * HD : (g + 1) * HD].astype(F32)
            for ref in (pk_ref, pv_ref)
            for g in range(2)
        ],
        axis=0,
    )

    barrier = pltpu.get_barrier_semaphore()
    greeted = [device(zl=a, zh=b) for a, b in z_partners]
    greeted += [device(y=a, core=b) for a, b in yc_partners]
    greeted += [device(x=a) for a in x_partners]
    for to in greeted:
        pl.semaphore_signal(barrier, inc=1, device_id=to, device_id_type=MESH)
    pl.semaphore_wait(barrier, len(greeted))

    pieces = [
        send(pz.at[mine_z], pz.at[mine_z], sem_pz, (i,), device(zl=a, zh=b))
        for i, (a, b) in enumerate(z_partners)
    ]

    for copy in packed:
        copy.wait()
    left_first = send(kvz.at[zh, 0], kvz.at[zh, 0], sem_z, (0,), device(zh=right))
    right_first = send(kvz.at[zh, 1], kvz.at[zh, 1], sem_z, (1,), device(zh=left))

    takers = [
        (j, b, 2 * core + j, jnp.logical_and(y == 2 * core + j, core == b))
        for j in range(2)
        for b in range(NC)
    ]

    def spread(step):
        zs = place_of[step]
        for i, (j, b, a, here) in enumerate(takers):
            deliver(
                kvz.at[zs, j, b], kva.at[zs, b, y],
                sem_kvs.at[step, i], sem_kvr.at[step, y], device(y=a, core=b), here,
            )

    def swap(step):
        zs = place_of[step]
        for a in range(NY):
            delivered(kva.at[zs, core, a], sem_kvr.at[step, a])
        return send(kva.at[zs, core], kva.at[zs, core], sem_ex, (step,), device(core=1 - core))

    for i, (j, b, a, here) in enumerate(takers):
        deliver(
            q_ref.at[:, pl.ds((j * NC + b) * LANES, LANES)], qb.at[y],
            sem_qs.at[i], sem_qr.at[y], device(y=a, core=b), here,
        )
    spread(OWN)
    grads_in = [
        send(
            g_ref.at[:, cols(a * (NC * LANES) + b * LANES, LANES)],
            gb.at[y, rows(core * HALF, HALF)],
            sem_g,
            (i,),
            device(y=a, core=b),
        )
        for i, (a, b) in enumerate(yc_partners)
    ]
    left_second = send(kvz.at[zh, 1], kvz.at[zh, 1], sem_z, (2,), device(zh=right))
    right_second = send(kvz.at[zh, 0], kvz.at[zh, 0], sem_z, (3,), device(zh=left))

    for copy in pieces:
        copy.wait_recv()
    mine_x = pl.ds(pl.multiple_of(x * 32, 32), 32)
    for t in range(4):
        for k in range(2):
            piece = pz[pl.ds(t * 2 + k, NZ, stride=8), :].astype(BF16)
            px[t, pl.ds(pl.multiple_of(x * 32 + k * 16, 16), 16), :] = piece
    prompt_x = [
        send(px.at[:, mine_x], px.at[:, mine_x], sem_px, (i,), device(x=a))
        for i, a in enumerate(x_partners)
    ]

    left_first.wait_recv()
    far_0 = send(kvz.at[left, 0], kvz.at[left, 0], sem_z, (4,), device(zh=right))
    right_first.wait_recv()
    far_1 = send(kvz.at[right, 1], kvz.at[right, 1], sem_z, (5,), device(zh=left))

    swapped = [swap(OWN), None, None, None]
    for copy in prompt_x:
        copy.wait_recv()
    mine_y = pl.ds(pl.multiple_of(y * BLOCK, BLOCK), BLOCK)
    for i, (j, b, a, here) in enumerate(takers):
        deliver(
            px.at[2 * b + j], pkv.at[b, mine_y],
            sem_pys.at[i], sem_pyr.at[y], device(y=a, core=b), here,
        )

    left_second.wait_recv()
    spread(LEFT)
    right_second.wait_recv()
    spread(RIGHT)

    for a in range(NY):
        delivered(qb.at[a], sem_qr.at[a])
    for copy in grads_in:
        copy.wait_recv()
    own_grads.wait()
    length = len_ref[0]
    for yb in range(NY):
        pos = lax.broadcasted_iota(jnp.int32, (BLOCK, LANES), 0) + (yb * NZH + zh) * BLOCK
        gb[yb] = jnp.where(pos < length, gb[yb].astype(F32), 0.0).astype(BF16)
        tot[yb] = jnp.zeros((8, LANES), F32)
        rdot[yb] = jnp.zeros((8, LANES), F32)
        dqt[yb] = jnp.zeros((HD, LANES), F32)

    key_at = lax.broadcasted_iota(jnp.int32, (BLOCK, LANES), 0)
    query_at = lax.broadcasted_iota(jnp.int32, (BLOCK, LANES), 1) % BLOCK
    gap = key_at - query_at

    def response_keys(step):
        return lambda c: kva[place_of[step], 0, c]

    def response_values(step):
        return lambda c: kva[place_of[step], 1, c]

    def prompt_keys(c):
        return pkv[0, pl.ds(c * BLOCK, BLOCK), :]

    def prompt_values(c):
        return pkv[1, pl.ds(c * BLOCK, BLOCK), :]

    def first_pass(yb, keys, values, count, e_ref, w_ref, d_ref, base, limit):
        queries, grads = stack_heads(qb[yb]), stack_heads(gb[yb])
        total, row_dot = tot[yb], rdot[yb]
        for c in range(count):
            score = dot_rows(keys(c), queries)
            grad_prob = dot_rows(values(c), grads)
            tangent = jnp.tanh(score * SCORE_FACTOR)
            weight = jnp.exp2(tangent * EXP2_FACTOR)
            if limit is not None and c == count - 1:
                weight = jnp.where(gap <= limit, weight, 0.0)
            slope = weight * (1.0 - tangent * tangent)
            total = total + weight.reshape(BLOCK // 8, 8, LANES).sum(0)
            row_dot = row_dot + (weight * grad_prob).reshape(BLOCK // 8, 8, LANES).sum(0)
            to = pl.ds(base + c * BLOCK, BLOCK)
            e_ref[to, :] = weight.astype(BF16)
            w_ref[to, :] = slope.astype(BF16)
            d_ref[to, :] = grad_prob.astype(BF16)
        tot[yb] = total
        rdot[yb] = row_dot

    def response_first(step):
        zs = place_of[step]
        limit = (zh - zs) * BLOCK
        swapped[step].wait_recv()
        for yb in range(NY):
            first_pass(
                yb, response_keys(step), response_values(step), yb + 1,
                er.at[step], wr.at[step], dr.at[step], BASE[yb], limit,
            )

    response_first(OWN)
    for a in range(NY):
        delivered(pkv.at[core, pl.ds(a * BLOCK, BLOCK)], sem_pyr.at[a])
    swapped_prompt = send(pkv.at[core], pkv.at[core], sem_ex, (4,), device(core=1 - core))
    swapped[LEFT] = swap(LEFT)
    swapped[RIGHT] = swap(RIGHT)

    swapped_prompt.wait_recv()
    for yb in range(NY):
        first_pass(
            yb, prompt_keys, prompt_values, PROMPT // BLOCK,
            ep.at[yb], wp.at[yb], dp.at[yb], 0, None,
        )

    far_0.wait_recv()
    far_1.wait_recv()
    spread(FAR)
    response_first(LEFT)
    response_first(RIGHT)
    swapped[FAR] = swap(FAR)
    response_first(FAR)

    for yb in range(NY):
        total = jnp.sum(tot[yb], axis=0, keepdims=True)
        row_dot = jnp.sum(rdot[yb], axis=0, keepdims=True)
        inverse = 1.0 / total
        tot[yb] = jnp.broadcast_to(inverse, (8, LANES))
        rdot[yb] = jnp.broadcast_to(row_dot * inverse, (8, LANES))

    def second_pass(yb, keys, count, e_ref, w_ref, d_ref, base, fresh, acc):
        queries, grads = stack_heads(qb[yb]), stack_heads(gb[yb])
        inverse = tot[yb, 0:1, :]
        inverse_root = inverse * INV_ROOT
        row_dot = rdot[yb, 0:1, :]
        query_grad = dqt[yb]
        for c in range(count):
            at = pl.ds(base + c * BLOCK, BLOCK)
            to = pl.ds(c * BLOCK, BLOCK)
            prob = (e_ref[at, :].astype(F32) * inverse).astype(BF16)
            grad_score = (
                (w_ref[at, :].astype(F32) * inverse_root) * (d_ref[at, :].astype(F32) - row_dot)
            ).astype(BF16)
            key_grad = dot(grad_score, queries)
            value_grad = dot(prob, grads)
            query_grad = query_grad + dot_first(keys(c), grad_score)
            if fresh(c):
                acc[0, to, :] = key_grad
                acc[1, to, :] = value_grad
            else:
                acc[0, to, :] += key_grad
                acc[1, to, :] += value_grad
        dqt[yb] = query_grad

    def trade(step):
        return send(acc.at[step, 1 - core], other.at[step], sem_rx, (step,), device(core=1 - core))

    partials = [None] * 4
    traded = [None] * 5

    def response_second(step):
        for yb in range(NY):
            second_pass(
                yb, response_keys(step), yb + 1,
                er.at[step], wr.at[step], dr.at[step], BASE[yb], lambda c, yb=yb: c == yb,
                acc.at[step],
            )
        traded[step] = trade(step)

    def hand_out(step):
        traded[step].wait_recv()
        send_kv[step] = (acc[step, core] + other[step]).astype(BF16)
        partials[step] = [
            send(
                send_kv.at[step, rows(a * BLOCK + b * HALF, HALF)],
                recv_kv.at[step, core, y],
                sem_rs,
                (step, i),
                device(y=a, core=b),
            )
            for i, (a, b) in enumerate(yc_partners)
        ]
        recv_kv[step, core, y] = send_kv[step, rows(y * BLOCK + core * HALF, HALF), :]

    def collect(step):
        for copy in partials[step]:
            copy.wait_recv()

    response_second(FAR)

    for yb in range(NY):
        second_pass(
            yb, prompt_keys, PROMPT // BLOCK, ep.at[yb], wp.at[yb], dp.at[yb], 0,
            lambda c, yb=yb: yb == 0, acc.at[4],
        )
    traded[4] = trade(4)
    hand_out(FAR)
    response_second(LEFT)

    traded[4].wait_recv()
    send_p[...] = acc[4, core] + other[4]
    for a in range(NY):
        deliver(
            send_p.at[pl.ds(a * BLOCK, BLOCK)], part_p.at[2 * core + y % 2],
            sem_sps.at[a], sem_spr.at[2 * core + y % 2], device(y=a, core=y // 2),
            jnp.logical_and(y == a, core == y // 2),
        )
    collect(FAR)
    far_key = send(recv_kv.at[FAR, 0], recv_z.at[0], sem_zr, (0,), device(zh=right))
    far_value = send(recv_kv.at[FAR, 1], recv_z.at[1], sem_zr, (1,), device(zh=left))
    hand_out(LEFT)
    response_second(RIGHT)

    for t in range(4):
        delivered(part_p.at[t], sem_spr.at[t])
    prompt_x_back = [
        send(
            part_p.at[:, pl.ds(pl.multiple_of(a * 32, 32), 32)],
            recv_x.at[i],
            sem_sx,
            (i,),
            device(x=a),
        )
        for i, a in enumerate(x_partners)
    ]
    collect(LEFT)
    key_right = send(recv_kv.at[LEFT, 0], recv_z.at[4], sem_zr, (4,), device(zh=left))
    hand_out(RIGHT)
    response_second(OWN)

    for yb in range(NY):
        for h in range(4):
            at = pl.ds(h * HD, HD)
            out_q[yb, :, at] = dqt[yb, :, at].T.astype(BF16)
    query_back = [
        send(
            out_q.at[a, rows(b * HALF, HALF)],
            gq_ref.at[:, mine_g],
            sem_oq,
            (i,),
            device(y=a, core=b),
        )
        for i, (a, b) in enumerate(yc_partners)
    ]
    own_back = local(out_q.at[y, rows(core * HALF, HALF)], gq_ref.at[:, mine_g], 12)

    for copy in prompt_x_back:
        copy.wait_recv()
    for t in range(4):
        part = part_p[t, mine_x, :]
        for i in range(NX - 1):
            part = part + recv_x[i, t]
        for k in range(2):
            tile_p[pl.ds(t * 2 + k, NZ, stride=8), :] = part[k * 16 : (k + 1) * 16]
    tiles_back = [
        send(
            tile_p.at[pl.ds(pl.multiple_of((b * NZL + a) * 8, 8), 8)],
            recv_t.at[i],
            sem_st,
            (i,),
            device(zl=a, zh=b),
        )
        for i, (a, b) in enumerate(z_partners)
    ]

    collect(RIGHT)
    value_left = send(recv_kv.at[RIGHT, 1], recv_z.at[3], sem_zr, (3,), device(zh=right))
    hand_out(OWN)
    far_key.wait_recv()
    send_z[0] = (recv_kv[RIGHT, 0].astype(F32) + recv_z[0].astype(F32)).astype(BF16)
    key_left = send(send_z.at[0], recv_z.at[2], sem_zr, (2,), device(zh=right))
    far_value.wait_recv()
    send_z[1] = (recv_kv[LEFT, 1].astype(F32) + recv_z[1].astype(F32)).astype(BF16)
    value_right = send(send_z.at[1], recv_z.at[5], sem_zr, (5,), device(zh=left))

    collect(OWN)
    key_left.wait_recv()
    key_right.wait_recv()
    value_left.wait_recv()
    value_right.wait_recv()
    for which, ref, first, second in ((0, gk_ref, 2, 4), (1, gv_ref, 3, 5)):
        for a in range(NY):
            total = recv_kv[OWN, which, a].astype(F32) + recv_z[first, a].astype(F32)
            ref[:, pl.ds(a * HD, HD)] = (total + recv_z[second, a].astype(F32)).astype(BF16)

    for copy in tiles_back:
        copy.wait_recv()
    tile = tile_p[mine_z, :]
    for i in range(NZ - 1):
        tile = tile + recv_t[i]
    for which, ref in enumerate((gpk_ref, gpv_ref)):
        for g in range(2):
            at = 4 * which + 2 * g
            ref[:, pl.ds(g * HD, HD)] = tile[at : at + 2].astype(BF16)

    for copy in query_back:
        copy.wait_recv()
    own_back.wait()
    for copy in started:
        copy.wait_send()
    for copy, here in conditional:

        @pl.when(jnp.logical_not(here))
        def _(copy=copy):
            copy.wait_send()


def shards(queries, keys, values, prefix_keys, prefix_values, grad_out, lengths):
    vmem = pl.BlockSpec(memory_space=pltpu.VMEM)
    anywhere = pl.BlockSpec(memory_space=pl.ANY)
    smem = pl.BlockSpec(memory_space=pltpu.SMEM)

    def sems(*dims):
        return pltpu.SemaphoreType.DMA((2, *dims))

    grads = pl.pallas_call(
        kernel,
        out_shape=(
            jax.ShapeDtypeStruct((HALF, NC * NY * LANES), BF16),
            jax.ShapeDtypeStruct((HALF, 4 * HD), BF16),
            jax.ShapeDtypeStruct((HALF, 4 * HD), BF16),
            jax.ShapeDtypeStruct((2, 2 * HD), BF16),
            jax.ShapeDtypeStruct((2, 2 * HD), BF16),
        ),
        in_specs=[smem, anywhere, anywhere, anywhere, anywhere, vmem, vmem],
        out_specs=(anywhere, vmem, vmem, vmem, vmem),
        scratch_shapes=[
            pltpu.VMEM((NY, BLOCK, LANES), BF16),
            pltpu.VMEM((NY, BLOCK, LANES), BF16),
            pltpu.VMEM((NZH, 2, 2, BLOCK, HD), BF16),
            pltpu.VMEM((NZH, 2, NY, BLOCK, HD), BF16),
            pltpu.VMEM((NZ * 8, HD), F32),
            pltpu.VMEM((4, NX * 32, HD), BF16),
            pltpu.VMEM((2, PROMPT, HD), BF16),
            pltpu.VMEM((NY, PROMPT, LANES), BF16),
            pltpu.VMEM((NY, PROMPT, LANES), BF16),
            pltpu.VMEM((NY, PROMPT, LANES), BF16),
            pltpu.VMEM((NZH, SEEN, LANES), BF16),
            pltpu.VMEM((NZH, SEEN, LANES), BF16),
            pltpu.VMEM((NZH, SEEN, LANES), BF16),
            pltpu.VMEM((NY, 8, LANES), F32),
            pltpu.VMEM((NY, 8, LANES), F32),
            pltpu.VMEM((NY, HD, LANES), F32),
            pltpu.VMEM((5, 2, NY * BLOCK, HD), F32),
            pltpu.VMEM((5, NY * BLOCK, HD), F32),
            pltpu.VMEM((NZH, NY * BLOCK, HD), BF16),
            pltpu.VMEM((NZH, 2, NY, HALF, HD), BF16),
            pltpu.VMEM((2, NY, HALF, HD), BF16),
            pltpu.VMEM((6, NY, HALF, HD), BF16),
            pltpu.VMEM((PROMPT, HD), F32),
            pltpu.VMEM((4, NX * 32, HD), F32),
            pltpu.VMEM((NX - 1, 4, 32, HD), F32),
            pltpu.VMEM((NZ * 8, HD), F32),
            pltpu.VMEM((NZ - 1, 8, HD), F32),
            pltpu.VMEM((NY, BLOCK, LANES), BF16),
            sems(NZ - 1),
            sems(6),
            pltpu.SemaphoreType.DMA((4,)),
            pltpu.SemaphoreType.DMA((NY,)),
            sems(NY * NC - 1),
            pltpu.SemaphoreType.DMA((NZH, 4)),
            pltpu.SemaphoreType.DMA((NZH, NY)),
            sems(5),
            sems(NX - 1),
            pltpu.SemaphoreType.DMA((4,)),
            pltpu.SemaphoreType.DMA((NY,)),
            sems(5),
            sems(NZH, NY * NC - 1),
            sems(6),
            pltpu.SemaphoreType.DMA((NY,)),
            pltpu.SemaphoreType.DMA((4,)),
            sems(NX - 1),
            sems(NZ - 1),
            sems(NY * NC - 1),
            pltpu.SemaphoreType.DMA((13,)),
        ],
        compiler_params=pltpu.CompilerParams(
            collective_id=0, has_side_effects=True, vmem_limit_bytes=VMEM_BYTES
        ),
        name="attention_grads",
    )(lengths, queries[0], keys[0], values[0], grad_out[0], prefix_keys, prefix_values)

    return (grads[0][None], grads[1][None], grads[2][None], grads[3], grads[4])


def solution(mesh):
    in_specs = (
        P("resp", "pre", "head"),
        P("resp", "pre", "head"),
        P("resp", "pre", "head"),
        P(("resp", "pre"), "head"),
        P(("resp", "pre"), "head"),
        P("resp", ("pre", "head"), None),
        P("resp"),
    )
    out_specs = (
        P("resp", ("pre", "head"), None),
        P("resp", ("pre", "head"), None),
        P("resp", ("pre", "head"), None),
        P(("resp", "pre"), "head"),
        P(("resp", "pre"), "head"),
    )
    return jax.shard_map(shards, mesh=mesh, in_specs=in_specs, out_specs=out_specs, check_vma=False)
```

time: 99.2 us -> 89.4 us (0.901)
  Pallas kernels: 90.2 us -> 83.2 us
  local copies, waits for them, and re-layouts: 7.06 us -> 4.66 us
    pallas_call x1, Pallas kernels: 90.2 us -> 83.2 us  [shards(): pl.pallas_call(kernel, out_shape=(jax.ShapeDtypeStruct((HALF, NC * NY * L...]
    unnamed x15 -> x13, local copies, waits for them, and re-layouts: 6.49 us -> 4.66 us
where the time goes in v2:
time: 89.4 us; the launch traced here: 89.2 us
  Pallas kernels  83.2 us (93%)
  local copies, waits for them, and re-layouts  4.66 us (5%)
  between operations  1.3 us (1%)
    pallas_call x1, Pallas kernels, shards(): pl.pallas_call(kernel, out_shape=(jax.ShapeDtypeStruct((HALF, NC * NY * L...  83.2 us
    unnamed x13, local copies, waits for them, and re-layouts  4.66 us

profile of v2, /device:TPU:1, one launch (start us, length us, event | category | flops | bytes accessed | tf_op | source)
XLA Modules:
  0.0 89.2 jit_solution(14036445505492354875)
XLA Ops:
  1.3 83.2 %attention_grads.1 = (bf16[64,4096]{1,0:T(8,128)(2,1)}, bf16[64,512]{1,0:T(8,128)(2,1)}, bf16[64,512]{1,0:T(8,128)(2,1)}, bf16[2,256]{1,0:T(2,128)(2,1)}, bf16[2,256]{1,0:T(2,128)(2,1)}) custom-call(s32[1]{0:T(128)S(6)} %copy.17.len_ref, bf16[128,2048]{1,0:T(8,128)(2,1)} %bitcast.7, bf16[128,256]{1,0:T(8,128)(2,1)} %bitcast.10, bf16[128,256]{1,0:T(8,128)(2,1)} %bitcast.11, ...), custom_call_target="tpu_custom_call" | custom-call | tf_op jit(solution)/shard_map/attention_grads/pallas_call | solution.py:507
  84.5 0.0 copy-start.1
  84.5 1.9 %copy.18 = bf16[1,64,4096]{2,1,0:T(8,128)(2,1)} copy(bf16[1,64,4096]{2,1,0:T(8,128)(2,1)} %bitcast.9) | data formatting | bytes 1048576
  86.4 0.0 copy-done.1
  86.4 0.0 copy-start
  86.4 0.6 copy.19
  87.0 0.2 copy-done
  87.3 0.0 copy-start.3
  87.3 0.6 copy.20
  87.9 0.0 copy-done.3
  87.9 0.0 copy-start.2
  87.9 0.6 copy.21
  88.5 0.1 copy-done.2
  88.6 0.6 copy.22
Async XLA Ops:
  84.5 1.9 %copy-start.1 = (bf16[64,512]{1,0:T(8,128)(2,1)S(1)}, bf16[64,512]{1,0:T(8,128)(2,1)}, u32[]{:S(2)}) copy-start(bf16[64,512]{1,0:T(8,128)(2,1)} %get-tuple-element.11) | copy-start | bytes 196612
  86.4 0.9 copy-start
  87.3 0.7 copy-start.3
  87.9 0.7 copy-start.2

commit v3 on v2

--- a/solution.py
+++ b/solution.py
@@ -170,7 +170,8 @@
         zs = place_of[step]
         for i, (j, b, a, here) in enumerate(takers):
             deliver(
-                kvz.at[zs, j, b], kva.at[zs, b, y],
+                kvz.at[zs, j] if step == FAR else kvz.at[zs, j, b],
+                kva.at[zs, :, y] if step == FAR else kva.at[zs, b, y],
                 sem_kvs.at[step, i], sem_kvr.at[step, y], device(y=a, core=b), here,
             )
 
@@ -283,7 +284,11 @@
     def response_first(step):
         zs = place_of[step]
         limit = (zh - zs) * BLOCK
-        swapped[step].wait_recv()
+        if step == FAR:
+            for a in range(NY):
+                delivered(kva.at[zs, :, a], sem_kvr.at[step, a])
+        else:
+            swapped[step].wait_recv()
         for yb in range(NY):
             first_pass(
                 yb, response_keys(step), response_values(step), yb + 1,
@@ -309,7 +314,6 @@
     spread(FAR)
     response_first(LEFT)
     response_first(RIGHT)
-    swapped[FAR] = swap(FAR)
     response_first(FAR)
 
     for yb in range(NY):

time: 89.4 us -> 90.9 us (1.017)
  Pallas kernels: 83.2 us -> 84.7 us
    pallas_call x1, Pallas kernels: 83.2 us -> 84.7 us  [shards(): pl.pallas_call(kernel, out_shape=(jax.ShapeDtypeStruct((HALF, NC * NY * L...]
where the time goes in v3:
time: 90.9 us; the launch traced here: 90.6 us
  Pallas kernels  84.7 us (93%)
  local copies, waits for them, and re-layouts  4.66 us (5%)
  between operations  1.3 us (1%)
    pallas_call x1, Pallas kernels, shards(): pl.pallas_call(kernel, out_shape=(jax.ShapeDtypeStruct((HALF, NC * NY * L...  84.7 us
    unnamed x13, local copies, waits for them, and re-layouts  4.66 us

profile of v3, /device:TPU:1, one launch (start us, length us, event | category | flops | bytes accessed | tf_op | source)
XLA Modules:
  0.0 90.6 jit_solution(12038325336959454657)
XLA Ops:
  1.3 84.7 %attention_grads.1 = (bf16[64,4096]{1,0:T(8,128)(2,1)}, bf16[64,512]{1,0:T(8,128)(2,1)}, bf16[64,512]{1,0:T(8,128)(2,1)}, bf16[2,256]{1,0:T(2,128)(2,1)}, bf16[2,256]{1,0:T(2,128)(2,1)}) custom-call(s32[1]{0:T(128)S(6)} %copy.17.len_ref, bf16[128,2048]{1,0:T(8,128)(2,1)} %bitcast.7, bf16[128,256]{1,0:T(8,128)(2,1)} %bitcast.10, bf16[128,256]{1,0:T(8,128)(2,1)} %bitcast.11, ...), custom_call_target="tpu_custom_call" | custom-call | tf_op jit(solution)/shard_map/attention_grads/pallas_call | solution.py:511
  86.0 0.0 copy-start.1
  86.0 1.9 %copy.18 = bf16[1,64,4096]{2,1,0:T(8,128)(2,1)} copy(bf16[1,64,4096]{2,1,0:T(8,128)(2,1)} %bitcast.9) | data formatting | bytes 1048576
  87.9 0.0 copy-done.1
  87.9 0.0 copy-start
  87.9 0.6 copy.19
  88.5 0.2 copy-done
  88.7 0.0 copy-start.3
  88.7 0.6 copy.20
  89.4 0.0 copy-done.3
  89.4 0.0 copy-start.2
  89.4 0.6 copy.21
  90.0 0.1 copy-done.2
  90.1 0.6 copy.22
Async XLA Ops:
  86.0 1.9 %copy-start.1 = (bf16[64,512]{1,0:T(8,128)(2,1)S(1)}, bf16[64,512]{1,0:T(8,128)(2,1)}, u32[]{:S(2)}) copy-start(bf16[64,512]{1,0:T(8,128)(2,1)} %get-tuple-element.11) | copy-start | bytes 196612
  87.9 0.9 copy-start
  88.7 0.7 copy-start.3
  89.4 0.7 copy-start.2
